TPU v7x, 512 devices: a whole 4x8x8 slice. The times are simulated.
512 devices in a mesh: patch: 64 (over z, y_lo, core), head: 8 (over y_hi, x).
Axes of the slice: x: 4, y: 8 (y_hi: 2, y_lo: 4; y = y_hi * 4 + y_lo), z: 8, core: 2. Of those that a mesh axis runs over, the one named last changes fastest.
Arguments:
- query_first: bfloat16 [4096, 3072], P(('patch', 'head')), may hold values from -256 to 256
- key_first: bfloat16 [4096, 3072], P(('patch', 'head')), may hold values from -8 to 8
- value_first: bfloat16 [4096, 3072], P(('patch', 'head')), may hold values from -6 to 6
- query_second: bfloat16 [4096, 3072], P(('patch', 'head')), may hold values from -256 to 256
- key_second: bfloat16 [4096, 3072], P(('patch', 'head')), may hold values from -6 to 6
- value_second: bfloat16 [4096, 3072], P(('patch', 'head')), may hold values from -6 to 6
- key_stale: bfloat16 [4096, 3072], P('patch', 'head'), may hold values from -8 to 8
- value_stale: bfloat16 [4096, 3072], P('patch', 'head'), may hold values from -6 to 6
- gate_table: float32 [50, 3072], P(None, 'head'), may hold values from 4 to 40
- step_index: int32 [2], replicated, may hold values from 0 to 49
Outputs:
- out_first: bfloat16 [4096, 3072], P(('patch', 'head'))
- out_second: bfloat16 [4096, 3072], P(('patch', 'head'))
All inputs are finite; a program needn't handle non-finite values.
Results may differ from a plain program's by a relative error of at most 0.0054.
Values may be sent and summed in bfloat16 or wider, within the bound.
No kernel may reach another device: no remote copies, remote signals or barrier semaphores. Data moves between devices by JAX's collectives and lax.ppermute only.
A program may use at most 64 MiB of HBM per device.

v0:
```python
import jax
import jax.numpy as jnp
from jax import lax
from jax.sharding import PartitionSpec as P

HDIM = 128


def pick_gate(gate_table, step_index, which):
    selector = jnp.arange(gate_table.shape[0], dtype=jnp.int32) == step_index[which]
    return jnp.sum(jnp.where(selector[:, None], gate_table, 0.0), axis=0)


def head_cols(block, which):
    return block[:, which * HDIM : (which + 1) * HDIM]


def pair_scores(left, right):
    return jnp.einsum("qd,kd->qk", left, right, preferred_element_type=jnp.float32) * HDIM ** (-0.5)


def attend_gathered(queries, fresh_keys, fresh_values, all_keys, all_values, own_start, gate_row):
    rows = queries.shape[0]
    ids = jnp.arange(all_keys.shape[0], dtype=jnp.int32)
    mine = (ids >= own_start) & (ids < own_start + rows)
    outputs = []
    for which in range(queries.shape[1] // HDIM):
        query_head = head_cols(queries, which)
        stale_scores = pair_scores(query_head, head_cols(all_keys, which))
        stale_scores = jnp.where(mine[None, :], -jnp.inf, stale_scores)
        own_scores = pair_scores(query_head, head_cols(fresh_keys, which))
        top = jnp.maximum(jnp.max(stale_scores, axis=1), jnp.max(own_scores, axis=1))
        stale_weights = jnp.exp(stale_scores - top[:, None])
        own_weights = jnp.exp(own_scores - top[:, None])
        total = jnp.sum(stale_weights, axis=1) + jnp.sum(own_weights, axis=1)
        acc = jnp.dot(
            stale_weights.astype(jnp.bfloat16),
            head_cols(all_values, which),
            preferred_element_type=jnp.float32,
        )
        acc = acc + jnp.dot(
            own_weights.astype(jnp.bfloat16),
            head_cols(fresh_values, which),
            preferred_element_type=jnp.float32,
        )
        outputs.append(acc / total[:, None])
    mixed = jnp.concatenate(outputs, axis=1)
    return (mixed * gate_row).astype(jnp.bfloat16)


def attend_both(first_in, second_in, key_stale, value_stale, gate_one, gate_two):
    rows = first_in[0].shape[0]
    own_start = lax.axis_index("patch") * rows
    all_keys, all_values = (
        lax.all_gather(key_stale, "patch", axis=0, tiled=True),
        lax.all_gather(value_stale, "patch", axis=0, tiled=True),
    )
    first = attend_gathered(
        first_in[0], first_in[1], first_in[2], all_keys, all_values, own_start, gate_one
    )
    second = attend_gathered(
        second_in[0], second_in[1], second_in[2], all_keys, all_values, own_start, gate_two
    )
    return (first, second)


def to_heads(queries, keys, values):
    return (
        lax.all_to_all(queries, "head", split_axis=1, concat_axis=0, tiled=True),
        lax.all_to_all(keys, "head", split_axis=1, concat_axis=0, tiled=True),
        lax.all_to_all(values, "head", split_axis=1, concat_axis=0, tiled=True),
    )


def to_tokens(result):
    return lax.all_to_all(result, "head", split_axis=0, concat_axis=1, tiled=True)


def body(
    query_first,
    key_first,
    value_first,
    query_second,
    key_second,
    value_second,
    key_stale,
    value_stale,
    gate_table,
    step_index,
):
    gate_one = pick_gate(gate_table, step_index, 0)
    gate_two = pick_gate(gate_table, step_index, 1)
    first_in = to_heads(query_first, key_first, value_first)
    second_in = to_heads(query_second, key_second, value_second)
    first, second = attend_both(first_in, second_in, key_stale, value_stale, gate_one, gate_two)
    out_first = to_tokens(first)
    out_second = to_tokens(second)
    return (out_first, out_second)


def solution(mesh):
    return jax.shard_map(
        body,
        mesh=mesh,
        in_specs=(
            P(("patch", "head"), None),
            P(("patch", "head"), None),
            P(("patch", "head"), None),
            P(("patch", "head"), None),
            P(("patch", "head"), None),
            P(("patch", "head"), None),
            P("patch", "head"),
            P("patch", "head"),
            P(None, "head"),
            P(),
        ),
        out_specs=(P(("patch", "head"), None), P(("patch", "head"), None)),
        check_vma=False,
    )
```

profile of v0, /device:TPU:1, one launch (start us, length us, event | category | flops | bytes accessed | tf_op | source)
XLA Modules:
  0.0 315.6 jit_solution(9896390958801457730)
XLA Ops:
  8.6 10.1 %all-to-all-start.4 = ((bf16[8,8,384]{2,0,1:T(8,128)(2,1)}), bf16[8,8,384]{2,0,1:T(8,128)(2,1)S(1)}, u32[]{:S(2)}, u32[]{:S(2)}) async-start(bf16[8,8,384]{2,0,1:T(8,128)(2,1)} %bitcast.64), calls=%async_computation.4 | async-start | bytes 98304 | tf_op jit(solution)/shard_map/all_to_all | solution.py:69
  18.8 1.3 fusion.111
  22.4 5.6 %all-to-all-done.4 = bf16[8,8,384]{2,0,1:T(8,128)(2,1)S(1)} async-done(((bf16[8,8,384]{2,0,1:T(8,128)(2,1)}), bf16[8,8,384]{2,0,1:T(8,128)(2,1)S(1)}, u32[]{:S(2)}, u32[]{:S(2)}) %all-to-all-start.4) | async-done | bytes 49184 | tf_op jit(solution)/shard_map/all_to_all | solution.py:69
  27.9 3.5 %all-to-all-start.5 = ((bf16[8,8,384]{2,0,1:T(8,128)(2,1)}), bf16[8,8,384]{2,0,1:T(8,128)(2,1)S(1)}, u32[]{:S(2)}, u32[]{:S(2)}) async-start(bf16[8,8,384]{2,0,1:T(8,128)(2,1)} %bitcast.65), calls=%async_computation.5 | async-start | bytes 98304 | tf_op jit(solution)/shard_map/all_to_all | solution.py:70
  31.5 9.1 %all-to-all-done.5 = bf16[8,8,384]{2,0,1:T(8,128)(2,1)S(1)} async-done(((bf16[8,8,384]{2,0,1:T(8,128)(2,1)}), bf16[8,8,384]{2,0,1:T(8,128)(2,1)S(1)}, u32[]{:S(2)}, u32[]{:S(2)}) %all-to-all-start.5) | async-done | bytes 49184 | tf_op jit(solution)/shard_map/all_to_all | solution.py:70
  40.5 3.4 %all-to-all-start = ((bf16[8,8,384]{2,0,1:T(8,128)(2,1)}), bf16[8,8,384]{2,0,1:T(8,128)(2,1)S(1)}, u32[]{:S(2)}, u32[]{:S(2)}) async-start(bf16[8,8,384]{2,0,1:T(8,128)(2,1)} %bitcast.66), calls=%async_computation | async-start | bytes 98304 | tf_op jit(solution)/shard_map/all_to_all | solution.py:69
  44.2 8.7 %all-to-all-done = bf16[8,8,384]{2,0,1:T(8,128)(2,1)S(1)} async-done(((bf16[8,8,384]{2,0,1:T(8,128)(2,1)}), bf16[8,8,384]{2,0,1:T(8,128)(2,1)S(1)}, u32[]{:S(2)}, u32[]{:S(2)}) %all-to-all-start) | async-done | bytes 49184 | tf_op jit(solution)/shard_map/all_to_all | solution.py:69
  52.9 3.3 %all-to-all-start.1 = ((bf16[8,8,384]{2,0,1:T(8,128)(2,1)}), bf16[8,8,384]{2,0,1:T(8,128)(2,1)S(1)}, u32[]{:S(2)}, u32[]{:S(2)}) async-start(bf16[8,8,384]{2,0,1:T(8,128)(2,1)} %bitcast.67), calls=%async_computation.1 | async-start | bytes 98304 | tf_op jit(solution)/shard_map/all_to_all | solution.py:70
  56.4 8.8 %all-to-all-done.1 = bf16[8,8,384]{2,0,1:T(8,128)(2,1)S(1)} async-done(((bf16[8,8,384]{2,0,1:T(8,128)(2,1)}), bf16[8,8,384]{2,0,1:T(8,128)(2,1)S(1)}, u32[]{:S(2)}, u32[]{:S(2)}) %all-to-all-start.1) | async-done | bytes 49184 | tf_op jit(solution)/shard_map/all_to_all | solution.py:70
  65.2 3.3 %all-to-all-start.6 = ((bf16[8,8,384]{2,0,1:T(8,128)(2,1)}), bf16[8,8,384]{2,0,1:T(8,128)(2,1)S(1)}, u32[]{:S(2)}, u32[]{:S(2)}) async-start(bf16[8,8,384]{2,0,1:T(8,128)(2,1)} %bitcast.68), calls=%async_computation.6 | async-start | bytes 98304 | tf_op jit(solution)/shard_map/all_to_all | solution.py:71
  69.6 64.9 %all-gather.3.cloned.1.call-done = bf16[4096,384]{1,0:T(8,128)(2,1)} async-done(((bf16[64,384]{1,0:T(8,128)(2,1)}), bf16[4096,384]{1,0:T(8,128)(2,1)}) %all-gather.3.cloned.1.call-update) | async-done | bytes 3145744 | tf_op jit(solution)/shard_map/all_gather | solution.py:55
  134.5 2.0 fusion.122
  145.1 109.1 %all-gather.5.cloned.1.call-done = bf16[4096,384]{1,0:T(8,128)(2,1)} async-done(((bf16[64,384]{1,0:T(8,128)(2,1)}), bf16[4096,384]{1,0:T(8,128)(2,1)}) %all-gather.5.cloned.1.call-update) | async-done | bytes 3145744 | tf_op jit(solution)/shard_map/all_gather | solution.py:56
  254.2 2.1 fusion.42
  256.9 8.9 %all-to-all-start.2 = ((bf16[8,8,384]{2,0,1:T(8,128)(2,1)}), bf16[8,8,384]{2,0,1:T(8,128)(2,1)S(1)}, u32[]{:S(2)}, u32[]{:S(2)}) async-start(bf16[8,8,384]{2,0,1:T(8,128)(2,1)} %bitcast.6), calls=%async_computation.2 | async-start | bytes 98304 | tf_op jit(solution)/shard_map/all_to_all | solution.py:71
  266.6 1.9 fusion.36
  270.1 1.6 fusion.30
  272.6 1.8 fusion.112
  275.9 9.0 %all-to-all-start.7 = ((bf16[8,8,384]{2,1,0:T(8,128)(2,1)}), bf16[8,8,384]{2,1,0:T(8,128)(2,1)S(1)}, u32[]{:S(2)}, u32[]{:S(2)}) async-start(bf16[8,8,384]{2,1,0:T(8,128)(2,1)} %fusion.61), calls=%async_computation.7 | async-start | bytes 98304 | tf_op jit(solution)/shard_map/all_to_all | solution.py:76
  285.1 1.6 fusion.38
  286.9 1.6 fusion.32
  289.4 4.6 %all-to-all-done.7 = bf16[8,8,384]{2,1,0:T(8,128)(2,1)S(1)} async-done(((bf16[8,8,384]{2,1,0:T(8,128)(2,1)}), bf16[8,8,384]{2,1,0:T(8,128)(2,1)S(1)}, u32[]{:S(2)}, u32[]{:S(2)}) %all-to-all-start.7) | async-done | bytes 49184 | tf_op jit(solution)/shard_map/all_to_all | solution.py:76
  294.0 4.4 %all-to-all-start.3 = ((bf16[8,8,384]{2,1,0:T(8,128)(2,1)}), bf16[8,8,384]{2,1,0:T(8,128)(2,1)S(1)}, u32[]{:S(2)}, u32[]{:S(2)}) async-start(bf16[8,8,384]{2,1,0:T(8,128)(2,1)} %fusion.60), calls=%async_computation.3 | async-start | bytes 98304 | tf_op jit(solution)/shard_map/all_to_all | solution.py:76
  298.4 9.1 %all-to-all-done.3 = bf16[8,8,384]{2,1,0:T(8,128)(2,1)S(1)} async-done(((bf16[8,8,384]{2,1,0:T(8,128)(2,1)}), bf16[8,8,384]{2,1,0:T(8,128)(2,1)S(1)}, u32[]{:S(2)}, u32[]{:S(2)}) %all-to-all-start.3) | async-done | bytes 49184 | tf_op jit(solution)/shard_map/all_to_all | solution.py:76
  (78 shorter events, 21.4 us)
Async XLA Ops:
  7.2 127.3 %all-gather.3.cloned.1.call-start = ((), (), s32[]{:S(2)}) async-start(), calls=%async_computation.8 | async-start | bytes 3194880 | tf_op jit(solution)/shard_map/all_gather | solution.py:55
  7.9 246.3 %all-gather.5.cloned.1.call-start = ((), (), s32[]{:S(2)}) async-start(), calls=%async_computation.9 | async-start | bytes 3194880 | tf_op jit(solution)/shard_map/all_gather | solution.py:56
  8.6 19.3 %all-to-all-start.4 = ((bf16[8,8,384]{2,0,1:T(8,128)(2,1)}), bf16[8,8,384]{2,0,1:T(8,128)(2,1)S(1)}, u32[]{:S(2)}, u32[]{:S(2)}) async-start(bf16[8,8,384]{2,0,1:T(8,128)(2,1)} %bitcast.64), calls=%async_computation.4 | async-start | bytes 98304 | tf_op jit(solution)/shard_map/all_to_all | solution.py:69
  27.9 12.6 %all-to-all-start.5 = ((bf16[8,8,384]{2,0,1:T(8,128)(2,1)}), bf16[8,8,384]{2,0,1:T(8,128)(2,1)S(1)}, u32[]{:S(2)}, u32[]{:S(2)}) async-start(bf16[8,8,384]{2,0,1:T(8,128)(2,1)} %bitcast.65), calls=%async_computation.5 | async-start | bytes 98304 | tf_op jit(solution)/shard_map/all_to_all | solution.py:70
  40.5 12.3 %all-to-all-start = ((bf16[8,8,384]{2,0,1:T(8,128)(2,1)}), bf16[8,8,384]{2,0,1:T(8,128)(2,1)S(1)}, u32[]{:S(2)}, u32[]{:S(2)}) async-start(bf16[8,8,384]{2,0,1:T(8,128)(2,1)} %bitcast.66), calls=%async_computation | async-start | bytes 98304 | tf_op jit(solution)/shard_map/all_to_all | solution.py:69
  52.9 12.3 %all-to-all-start.1 = ((bf16[8,8,384]{2,0,1:T(8,128)(2,1)}), bf16[8,8,384]{2,0,1:T(8,128)(2,1)S(1)}, u32[]{:S(2)}, u32[]{:S(2)}) async-start(bf16[8,8,384]{2,0,1:T(8,128)(2,1)} %bitcast.67), calls=%async_computation.1 | async-start | bytes 98304 | tf_op jit(solution)/shard_map/all_to_all | solution.py:70
  65.2 191.7 %all-to-all-start.6 = ((bf16[8,8,384]{2,0,1:T(8,128)(2,1)}), bf16[8,8,384]{2,0,1:T(8,128)(2,1)S(1)}, u32[]{:S(2)}, u32[]{:S(2)}) async-start(bf16[8,8,384]{2,0,1:T(8,128)(2,1)} %bitcast.68), calls=%async_computation.6 | async-start | bytes 98304 | tf_op jit(solution)/shard_map/all_to_all | solution.py:71
  134.5 3.5 %copy-start.1 = (bf16[4096,384]{1,0:T(8,128)(2,1)S(1)}, bf16[4096,384]{1,0:T(8,128)(2,1)}, u32[]{:S(2)}) copy-start(bf16[4096,384]{1,0:T(8,128)(2,1)} %all-gather.3.cloned.1.call-done) | copy-start | bytes 9437188
  136.4 1.0 copy-start.7
  138.6 1.6 copy-start.5
  140.1 4.1 %copy-start.6 = (f32[64,4096]{1,0:T(8,128)}, f32[64,4096]{1,0:T(8,128)S(1)}, u32[]{:S(2)}) copy-start(f32[64,4096]{1,0:T(8,128)S(1)} %get-tuple-element.19) | copy-start | bytes 3145732
  140.7 2.6 copy-start.3
  141.3 2.9 copy-start.2
  254.2 15.9 %copy-start = (bf16[4096,384]{1,0:T(8,128)(2,1)S(1)}, bf16[4096,384]{1,0:T(8,128)(2,1)}, u32[]{:S(2)}) copy-start(bf16[4096,384]{1,0:T(8,128)(2,1)} %all-gather.5.cloned.1.call-done) | copy-start | bytes 9437188
  256.9 19.0 %all-to-all-start.2 = ((bf16[8,8,384]{2,0,1:T(8,128)(2,1)}), bf16[8,8,384]{2,0,1:T(8,128)(2,1)S(1)}, u32[]{:S(2)}, u32[]{:S(2)}) async-start(bf16[8,8,384]{2,0,1:T(8,128)(2,1)} %bitcast.6), calls=%async_computation.2 | async-start | bytes 98304 | tf_op jit(solution)/shard_map/all_to_all | solution.py:71
  265.8 6.8 %copy-start.9 = (f32[64]{0:T(128)S(1)}, f32[64]{0:T(128)}, u32[]{:S(2)}) copy-start(f32[64]{0:T(128)} %fusion.20) | copy-start | bytes 772
  265.8 6.8 %copy-start.11 = (f32[64]{0:T(128)S(1)}, f32[64]{0:T(128)}, u32[]{:S(2)}) copy-start(f32[64]{0:T(128)} %fusion.64) | copy-start | bytes 772
  266.6 7.8 %copy-start.10 = (f32[64]{0:T(128)S(1)}, f32[64]{0:T(128)}, u32[]{:S(2)}) copy-start(f32[64]{0:T(128)} %get-tuple-element.8) | copy-start | bytes 772
  268.6 6.9 %copy-start.4 = (f32[64,4096]{1,0:T(8,128)S(1)}, f32[64,4096]{1,0:T(8,128)}, u32[]{:S(2)}) copy-start(f32[64,4096]{1,0:T(8,128)} %copy-done.3) | copy-start | bytes 3145732
  274.4 1.4 copy-start.8
  275.9 18.1 %all-to-all-start.7 = ((bf16[8,8,384]{2,1,0:T(8,128)(2,1)}), bf16[8,8,384]{2,1,0:T(8,128)(2,1)S(1)}, u32[]{:S(2)}, u32[]{:S(2)}) async-start(bf16[8,8,384]{2,1,0:T(8,128)(2,1)} %fusion.61), calls=%async_computation.7 | async-start | bytes 98304 | tf_op jit(solution)/shard_map/all_to_all | solution.py:76
  294.0 13.5 %all-to-all-start.3 = ((bf16[8,8,384]{2,1,0:T(8,128)(2,1)}), bf16[8,8,384]{2,1,0:T(8,128)(2,1)S(1)}, u32[]{:S(2)}, u32[]{:S(2)}) async-start(bf16[8,8,384]{2,1,0:T(8,128)(2,1)} %fusion.60), calls=%async_computation.3 | async-start | bytes 98304 | tf_op jit(solution)/shard_map/all_to_all | solution.py:76
Sparse Core Ops, SparseCore 0:
  10.1 124.2 all-gather.2
  136.6 117.5 all-gather.4
where the time goes:
time: 318 us; the launch traced here: 316 us
  waiting for transfers between devices  221 us (69%)
  starting transfers between devices  46.1 us (14%)
  matrix products  19.2 us (6%)
  between operations  14.3 us (4%)
  other arithmetic  11.5 us (4%)
  local copies, waits for them, and re-layouts  3.21 us (1%)
    all_gather x1, waiting for transfers between devices, attend_both(): lax.all_gather(value_stale, 'patch', axis=0, tiled=True)  109 us
    all_gather x1, waiting for transfers between devices, attend_both(): lax.all_gather(key_stale, 'patch', axis=0, tiled=True)  64.9 us
    all_to_all x2, waiting for transfers between devices, to_heads(): lax.all_to_all(keys, 'head', split_axis=1, concat_axis=0, tiled=True)  17.9 us
    all_to_all x2, waiting for transfers between devices, to_heads(): lax.all_to_all(queries, 'head', split_axis=1, concat_axis=0, tiled=True)  14.2 us
    all_to_all x2, waiting for transfers between devices, to_tokens(): lax.all_to_all(result, 'head', split_axis=0, concat_axis=1, tiled=True)  13.7 us
    all_to_all x2, starting transfers between devices, to_heads(): lax.all_to_all(queries, 'head', split_axis=1, concat_axis=0, tiled=True)  13.5 us
    all_to_all x2, starting transfers between devices, to_tokens(): lax.all_to_all(result, 'head', split_axis=0, concat_axis=1, tiled=True)  13.5 us
    all_to_all x2, starting transfers between devices, to_heads(): lax.all_to_all(values, 'head', split_axis=1, concat_axis=0, tiled=True)  12.2 us
  transfers between devices with their start and end apart: 10, of which 8 were waited for; matrix products, arithmetic and copies ran while one was open for 10% of the time, Pallas kernels for 0%

commit v1 on v0

v1 whole, which is shorter than its diff:
```python
import functools

import jax
import jax.numpy as jnp
from jax import lax
from jax.experimental import pallas as pl
from jax.experimental.pallas import tpu as pltpu
from jax.sharding import Mesh
from jax.sharding import PartitionSpec as P

HDIM = 128
GROUP = 3
WIDTH = GROUP * HDIM
NZ, NY, NC, NH, NX = 8, 4, 2, 2, 4
NHEAD = NH * NX
PEERS = NY * NHEAD
TOK = 8
PATCH = TOK * NHEAD
FRESH = 2 * TOK // NY
BLOCK = 2 * TOK + 2 * FRESH
SCALE2 = HDIM ** (-0.5) * 1.4426950408889634
LN2 = 0.6931471805599453
NEG = -1e30
F32 = jnp.float32
BF16 = jnp.bfloat16
PLANE = ("y", "h", "x")


def pack_kernel(q1, k1, v1, q2, k2, v2, ks, vs, out, kv):
    kv[:, 0:WIDTH] = ks[...]
    kv[:, WIDTH : 2 * WIDTH] = vs[...]
    share = TOK // NY
    for g in range(NHEAD):
        cols = slice(g * WIDTH, (g + 1) * WIDTH)
        queries = jnp.concatenate([q1[:, cols].astype(F32), q2[:, cols].astype(F32)], axis=0).astype(BF16)
        fresh = [ref[:, cols].astype(F32) for ref in (k1, k2, v1, v2)]
        for y in range(NY):
            rows = slice(y * share, (y + 1) * share)
            part = jnp.concatenate([f[rows] for f in fresh], axis=0).astype(BF16)
            out[y * NHEAD + g, 0 : 2 * TOK, :] = queries
            out[y * NHEAD + g, 2 * TOK : BLOCK, :] = part


def split3(x):
    hi = x.astype(BF16)
    rest = x - hi.astype(F32)
    mid = rest.astype(BF16)
    lo = (rest - mid.astype(F32)).astype(BF16)
    return hi, mid, lo


def nt_dot(a, b):
    return lax.dot_general(a, b, (((1,), (1,)), ((), ())), preferred_element_type=F32)


def attend_kernel(where_ref, step_ref, recv, own, other, gates, out):
    my_z = where_ref[0]
    my_y = where_ref[1]
    keys = NZ * PATCH
    rows = 2 * PATCH
    fresh_rows = NHEAD * 2 * FRESH
    col = lax.broadcasted_iota(jnp.int32, (1, keys), 1)
    own_bias = jnp.where(col // PATCH == my_z, NEG, 0.0)
    q_step = (lax.broadcasted_iota(jnp.int32, (rows, fresh_rows), 0) // TOK) % 2
    f_kind = lax.broadcasted_iota(jnp.int32, (rows, fresh_rows), 1) % (2 * FRESH) // (FRESH // 2)
    fresh_bias = jnp.where(f_kind == q_step, 0.0, NEG)
    at = lax.broadcasted_iota(jnp.int32, (fresh_rows, fresh_rows), 0)
    to = lax.broadcasted_iota(jnp.int32, (fresh_rows, fresh_rows), 1)
    shift = jnp.where(to == at + FRESH, 1.0, 0.0).astype(BF16)
    gate0 = gates[pl.ds(step_ref[0], 1), :]
    gate1 = gates[pl.ds(step_ref[1], 1), :]
    lane = lax.broadcasted_iota(jnp.int32, (rows, HDIM), 1)
    step_of_row = (lax.broadcasted_iota(jnp.int32, (rows, HDIM), 0) // TOK) % 2
    for y in range(NY):
        blocks = slice(y * NHEAD, (y + 1) * NHEAD)
        bias = jnp.where(my_y == y, own_bias, 0.0)
        stats = jnp.zeros((rows, HDIM), F32)
        for head in range(GROUP):
            cols = slice(head * HDIM, (head + 1) * HDIM)
            vcols = slice(WIDTH + head * HDIM, WIDTH + (head + 1) * HDIM)
            q = recv[blocks, 0 : 2 * TOK, cols].reshape(rows, HDIM)
            fresh = recv[blocks, 2 * TOK : BLOCK, cols].astype(F32).reshape(fresh_rows, HDIM).astype(BF16)
            fresh_v = jnp.dot(shift, fresh, preferred_element_type=F32).astype(BF16)
            s_own = nt_dot(q, own[:, cols]) + bias
            s_other = nt_dot(q, other[:, cols])
            s_fresh = nt_dot(q, fresh) + fresh_bias
            top = jnp.maximum(
                jnp.maximum(jnp.max(s_own, axis=1, keepdims=True), jnp.max(s_other, axis=1, keepdims=True)),
                jnp.max(s_fresh, axis=1, keepdims=True),
            )
            p_own = jnp.exp2((s_own - top) * SCALE2)
            p_other = jnp.exp2((s_other - top) * SCALE2)
            p_fresh = jnp.exp2((s_fresh - top) * SCALE2)
            total = (
                jnp.sum(p_own, axis=1, keepdims=True)
                + jnp.sum(p_other, axis=1, keepdims=True)
                + jnp.sum(p_fresh, axis=1, keepdims=True)
            )
            acc = jnp.dot(p_own.astype(BF16), own[:, vcols], preferred_element_type=F32)
            acc = acc + jnp.dot(p_other.astype(BF16), other[:, vcols], preferred_element_type=F32)
            acc = acc + jnp.dot(p_fresh.astype(BF16), fresh_v, preferred_element_type=F32)
            gate = jnp.where(step_of_row == 0, gate0[:, cols], gate1[:, cols])
            mixed = (acc / total) * gate
            out[blocks, :, cols] = mixed.astype(BF16).reshape(NHEAD, 2 * TOK, HDIM)
            size = top * SCALE2 + jnp.log(total) * (1.0 / LN2)
            for i, piece in enumerate(split3(size)):
                stats = jnp.where(lane == 3 * head + i, piece.astype(F32), stats)
        out[blocks, :, WIDTH:] = stats.astype(BF16).reshape(NHEAD, 2 * TOK, HDIM)


def merge_kernel(recv, out_first, out_second):
    rows = NHEAD * 2 * TOK
    at = lax.broadcasted_iota(jnp.int32, (HDIM, WIDTH), 0)
    to = lax.broadcasted_iota(jnp.int32, (HDIM, WIDTH), 1)
    spread = jnp.where(at // 3 == to // HDIM, 1.0, 0.0).astype(BF16)
    sizes, parts = [], []
    for y in range(NY):
        blocks = slice(y * NHEAD, (y + 1) * NHEAD)
        stats = recv[blocks, :, WIDTH:].reshape(rows, HDIM)
        sizes.append(jnp.dot(stats, spread, preferred_element_type=F32))
        parts.append(recv[blocks, :, 0:WIDTH].reshape(rows, WIDTH).astype(F32))
    top = functools.reduce(jnp.maximum, sizes)
    total = jnp.zeros_like(top)
    acc = jnp.zeros_like(top)
    for size, part in zip(sizes, parts, strict=True):
        weight = jnp.exp2(size - top)
        total = total + weight
        acc = acc + weight * part
    result = acc / total
    for g in range(NHEAD):
        cols = slice(g * WIDTH, (g + 1) * WIDTH)
        out_first[:, cols] = result[g * 2 * TOK : g * 2 * TOK + TOK].astype(BF16)
        out_second[:, cols] = result[g * 2 * TOK + TOK : (g + 1) * 2 * TOK].astype(BF16)


def vmem(n):
    return [pl.BlockSpec(memory_space=pltpu.VMEM)] * n


def smem(n):
    return [pl.BlockSpec(memory_space=pltpu.SMEM)] * n


PARAMS = pltpu.CompilerParams(vmem_limit_bytes=40 * 1024 * 1024)


def body(q1, k1, v1, q2, k2, v2, key_stale, value_stale, gate_table, step_index):
    shape = jax.ShapeDtypeStruct
    packed, kv = pl.pallas_call(
        pack_kernel,
        out_shape=(shape((PEERS, BLOCK, WIDTH), BF16), shape((PATCH, 2 * WIDTH), BF16)),
        in_specs=vmem(8),
        out_specs=tuple(vmem(2)),
        compiler_params=PARAMS,
        name="pack",
    )(q1, k1, v1, q2, k2, v2, key_stale, value_stale)
    recv = lax.all_to_all(packed, PLANE, split_axis=0, concat_axis=0, tiled=True)
    own = lax.all_gather(kv, "z", axis=0, tiled=True)
    other = lax.ppermute(own, "c", [(0, 1), (1, 0)])
    where = jnp.stack([lax.axis_index("z"), lax.axis_index("y")]).astype(jnp.int32)
    partial = pl.pallas_call(
        attend_kernel,
        out_shape=shape((PEERS, 2 * TOK, WIDTH + HDIM), BF16),
        in_specs=smem(2) + vmem(4),
        out_specs=vmem(1)[0],
        compiler_params=PARAMS,
        name="attend",
    )(where, step_index, recv, own, other, gate_table)
    back = lax.all_to_all(partial, PLANE, split_axis=0, concat_axis=0, tiled=True)
    return pl.pallas_call(
        merge_kernel,
        out_shape=(shape((TOK, NHEAD * WIDTH), BF16),) * 2,
        in_specs=vmem(1),
        out_specs=tuple(vmem(2)),
        compiler_params=PARAMS,
        name="merge",
    )(back)


def solution(mesh):
    fine = Mesh(mesh.devices.reshape(NZ, NY, NC, NH, NX), ("z", "y", "c", "h", "x"))
    tokens = P(("z", "y", "c", "h", "x"), None)
    kept = P(("z", "y", "c"), ("h", "x"))
    return jax.shard_map(
        body,
        mesh=fine,
        in_specs=(tokens,) * 6 + (kept, kept, P(None, ("h", "x")), P()),
        out_specs=(tokens, tokens),
        check_vma=False,
    )
```

time: 318 us -> 90.9 us (0.29)
  waiting for transfers between devices: 221 us -> 1.8 us
  blocking collectives: 0 us -> 54.7 us
  starting transfers between devices: 46.1 us -> 17.9 us
  matrix products: 19.2 us -> 0 us
  between operations: 14.3 us -> 0.7 us
  other arithmetic: 11.5 us -> 0.08 us
  Pallas kernels: 0 us -> 8.06 us
    all_gather x2 -> x0, waiting for transfers between devices: 174 us -> none  [the longest x1 109 us: attend_both(): lax.all_gather(value_stale, 'patch', axis=0, tiled=True)]
    all_to_all x8 -> x1, waiting for transfers between devices: 45.9 us -> 0.01 us  [body(): lax.all_to_all(packed, PLANE, split_axis=0, concat_axis=0, tiled=True)]
    all_to_all x8 -> x1, starting transfers between devices: 46 us -> 10.5 us  [body(): lax.all_to_all(packed, PLANE, split_axis=0, concat_axis=0, tiled=True)]
    all_gather x0 -> x1, blocking collectives: none -> 28 us  [body(): own = lax.all_gather(kv, 'z', axis=0, tiled=True)]
    all_to_all x0 -> x1, blocking collectives: none -> 26.7 us  [body(): lax.all_to_all(partial, PLANE, split_axis=0, concat_axis=0, tiled=True)]
    dot_general x24 -> x0, matrix products: 19.2 us -> none  [the longest x6 9.17 us: attend_gathered(): jnp.dot(stale_weights.astype(jnp.bfloat16), head_cols(all_values, which),...]
    pallas_call x0 -> x3, Pallas kernels: none -> 8.06 us  [the longest x1 6.08 us: body(): pl.pallas_call(attend_kernel, out_shape=shape((PEERS, 2 * TOK, WIDTH + HD...]
    ppermute x0 -> x1, starting transfers between devices: none -> 7.44 us  [body(): other = lax.ppermute(own, 'c', [(0, 1), (1, 0)])]
  transfers between devices with their start and end apart: 10 -> 2, of which waited for: 8 -> 1; matrix products, arithmetic and copies ran while one was open for 10% -> 0% of each run, Pallas kernels for 0% -> 0%
where the time goes in v1:
time: 90.9 us; the launch traced here: 89.6 us
  blocking collectives  54.7 us (60%)
  starting transfers between devices  17.9 us (20%)
  Pallas kernels  8.06 us (9%)
  local copies, waits for them, and re-layouts  6.39 us (7%)
  waiting for transfers between devices  1.8 us (2%)
    all_gather x1, blocking collectives, body(): own = lax.all_gather(kv, 'z', axis=0, tiled=True)  28 us
    all_to_all x1, blocking collectives, body(): lax.all_to_all(partial, PLANE, split_axis=0, concat_axis=0, tiled=True)  26.7 us
    all_to_all x1, starting transfers between devices, body(): lax.all_to_all(packed, PLANE, split_axis=0, concat_axis=0, tiled=True)  10.5 us
    ppermute x1, starting transfers between devices, body(): other = lax.ppermute(own, 'c', [(0, 1), (1, 0)])  7.44 us
    unnamed x20, local copies, waits for them, and re-layouts  6.39 us
    pallas_call x1, Pallas kernels, body(): pl.pallas_call(attend_kernel, out_shape=shape((PEERS, 2 * TOK, WIDTH + HD...  6.08 us
  transfers between devices with their start and end apart: 2, of which 1 were waited for; matrix products, arithmetic and copies ran while one was open for 0% of the time, Pallas kernels for 0%

profile of v1, /device:TPU:1, one launch (start us, length us, event | category | flops | bytes accessed | tf_op | source)
XLA Modules:
  0.0 89.6 jit_solution(8268276851184459089)
XLA Ops:
  0.6 0.0 copy-start.1
  0.6 0.8 copy-done.1
  1.4 0.0 copy-start.2
  1.4 0.8 copy-done.2
  2.2 0.8 copy-done.3
  3.0 0.8 copy-done.4
  3.8 0.8 copy-done.5
  4.6 0.8 copy-done.6
  5.4 0.8 copy-done.7
  6.2 0.8 copy-done.8
  7.0 0.9 %pack.1 = (bf16[32,24,384]{2,1,0:T(8,128)(2,1)}, bf16[64,768]{1,0:T(8,128)(2,1)S(1)}) custom-call(bf16[8,3072]{1,0:T(8,128)(2,1)S(1)} %copy-done.1, bf16[8,3072]{1,0:T(8,128)(2,1)S(1)} %copy-done.2, bf16[8,3072]{1,0:T(8,128)(2,1)S(1)} %copy-done.3, bf16[8,3072]{1,0:T(8,128)(2,1)S(1)} %copy-done.4, bf16[8,3072]{1,0:T(8,128)(2,1)S(1)} %copy-done.5, ...), custom_call_target="tpu_custom_call" | custom-call | tf_op jit(solution)/shard_map/pack/pallas_call | solution.py:149
  8.0 10.5 %all-to-all-start = ((bf16[32,24,384]{2,1,0:T(8,128)(2,1)}), bf16[32,24,384]{2,1,0:T(8,128)(2,1)S(1)}, u32[]{:S(2)}, u32[]{:S(2)}) async-start(bf16[32,24,384]{2,1,0:T(8,128)(2,1)} %get-tuple-element.4), calls=%async_computation | async-start | bytes 1179648 | tf_op jit(solution)/shard_map/all_to_all | solution.py:157
  18.5 0.0 copy-start
  18.5 28.0 %all_gather.3.own = bf16[512,768]{1,0:T(8,128)(2,1)S(1)} all-gather(bf16[64,768]{1,0:T(8,128)(2,1)S(1)} %get-tuple-element.5), channel_id=1, replica_groups=mesh['z'=8,'y'=4,'c'=2,'h'=2,'x'=4] {'z'}, dimensions={0}, use_global_device_ids=true | all-gather | bytes 884736 | tf_op jit(solution)/shard_map/all_gather | solution.py:158
  46.5 7.4 %collective-permute-start = (bf16[512,768]{1,0:T(8,128)(2,1)S(1)}, bf16[512,768]{1,0:T(8,128)(2,1)S(1)}, u32[]{:S(2)}, u32[]{:S(2)}) collective-permute-start(bf16[512,768]{1,0:T(8,128)(2,1)S(1)} %all_gather.3.own), channel_id=1, source_target_pairs={{0,8},{8,0},{1,9},{9,1},{2,10},{10,2},{3,11},{11,3},{4,12},{12,4},... | collective-permute-start | bytes 2359304 | tf_op jit(solution)/shard_map/ppermute | solution.py:159
  53.9 0.0 copy-start.9
  53.9 0.1 pad_add_fusion.where_ref
  54.0 1.8 %collective-permute-done.other = bf16[512,768]{1,0:T(8,128)(2,1)S(1)} collective-permute-done((bf16[512,768]{1,0:T(8,128)(2,1)S(1)}, bf16[512,768]{1,0:T(8,128)(2,1)S(1)}, u32[]{:S(2)}, u32[]{:S(2)}) %collective-permute-start) | collective-permute-done | bytes 786464 | tf_op jit(solution)/shard_map/ppermute | solution.py:159
  55.8 0.0 all-to-all-done.recv
  55.8 0.0 copy-done
  55.8 0.0 copy-done.9
  55.8 6.1 %attend.1 = bf16[32,16,512]{2,1,0:T(8,128)(2,1)S(1)} custom-call(s32[2]{0:T(128)S(1)} %pad_add_fusion.where_ref, s32[2]{0:T(128)S(1)} %copy-done.9, bf16[32,24,384]{2,1,0:T(8,128)(2,1)S(1)} %all-to-all-done.recv, bf16[512,768]{1,0:T(8,128)(2,1)S(1)} %all_gather.3.own, bf16[512,768]{1,0:T(8,128)(2,1)S(1)} %collective-permute-done.other, f32[50,384]{1,0:T(8,128)S(1)} %copy-done), custom_call_target="tpu_custom_call" | custom-call | tf_op jit(solution)/shard_map/attend/pallas_call | solution.py:161
  61.9 26.7 %all_to_all.10.recv = bf16[32,16,512]{2,1,0:T(8,128)(2,1)S(1)} all-to-all(bf16[32,16,512]{2,1,0:T(8,128)(2,1)S(1)} %attend.1), channel_id=1, replica_groups=mesh['z'=8,'y'=4,'c'=2,'h'=2,'x'=4] {'y','h','x'}, dimensions={0} | all-to-all | bytes 1048576 | tf_op jit(solution)/shard_map/all_to_all | solution.py:169
  88.6 1.0 %merge.1 = (bf16[8,3072]{1,0:T(8,128)(2,1)}, bf16[8,3072]{1,0:T(8,128)(2,1)}) custom-call(bf16[32,16,512]{2,1,0:T(8,128)(2,1)S(1)} %all_to_all.10.recv), custom_call_target="tpu_custom_call" | custom-call | tf_op jit(solution)/shard_map/merge/pallas_call | solution.py:170
  (6 shorter events, 0.0 us)
Async XLA Ops:
  0.6 0.8 copy-start.1
  1.4 0.8 copy-start.2
  2.2 0.8 copy-start.3
  3.0 0.8 copy-start.4
  3.8 0.8 copy-start.5
  4.6 0.8 copy-start.6
  5.4 0.8 copy-start.7
  6.2 0.8 copy-start.8
  8.0 47.9 %all-to-all-start = ((bf16[32,24,384]{2,1,0:T(8,128)(2,1)}), bf16[32,24,384]{2,1,0:T(8,128)(2,1)S(1)}, u32[]{:S(2)}, u32[]{:S(2)}) async-start(bf16[32,24,384]{2,1,0:T(8,128)(2,1)} %get-tuple-element.4), calls=%async_computation | async-start | bytes 1179648 | tf_op jit(solution)/shard_map/all_to_all | solution.py:157
  18.5 37.4 %copy-start = (f32[50,384]{1,0:T(8,128)S(1)}, f32[50,384]{1,0:T(8,128)}, u32[]{:S(2)}) copy-start(f32[50,384]{1,0:T(8,128)} %gates.1) | copy-start | bytes 230404
  46.5 9.3 %collective-permute-start = (bf16[512,768]{1,0:T(8,128)(2,1)S(1)}, bf16[512,768]{1,0:T(8,128)(2,1)S(1)}, u32[]{:S(2)}, u32[]{:S(2)}) collective-permute-start(bf16[512,768]{1,0:T(8,128)(2,1)S(1)} %all_gather.3.own), channel_id=1, source_target_pairs={{0,8},{8,0},{1,9},{9,1},{2,10},{10,2},{3,11},{11,3},{4,12},{12,4},... | collective-permute-start | bytes 2359304 | tf_op jit(solution)/shard_map/ppermute | solution.py:159
  53.9 1.9 %copy-start.9 = (s32[2]{0:T(128)S(1)}, s32[2]{0:T(128)}, u32[]{:S(2)}) copy-start(s32[2]{0:T(128)} %step_ref.1) | copy-start | bytes 28

commit v2 on v1

v2 whole, which is shorter than its diff:
```python
import functools

import jax
import jax.numpy as jnp
from jax import lax
from jax.experimental import pallas as pl
from jax.experimental.pallas import tpu as pltpu
from jax.sharding import Mesh
from jax.sharding import PartitionSpec as P

HDIM = 128
GROUP = 3
WIDTH = GROUP * HDIM
NZ, NY, NC, NH, NX = 8, 4, 2, 2, 4
NHEAD = NH * NX
PEERS = NY * NHEAD
TOK = 8
PATCH = TOK * NHEAD
FRESH = 2 * TOK // NY
BLOCK = 2 * TOK + 2 * FRESH
SENT = 2 * TOK * GROUP + TOK
SCALE2 = HDIM ** (-0.5) * 1.4426950408889634
LN2 = 0.6931471805599453
NEG = -1e30
F32 = jnp.float32
BF16 = jnp.bfloat16
PLANE = ("y", "h", "x")


def pack_kernel(q1, k1, v1, q2, k2, v2, ks, vs, out, kv, b0, b1, b2, b3, b4, b5, sems):
    pairs = [(q1, b0), (q2, b1), (k1, b2), (k2, b3), (v1, b4), (v2, b5)]
    pairs += [(ks, kv.at[:, 0:WIDTH]), (vs, kv.at[:, WIDTH : 2 * WIDTH])]
    copies = [pltpu.make_async_copy(src, dst, sems.at[i]) for i, (src, dst) in enumerate(pairs)]
    for copy in copies:
        copy.start()
    share = TOK // NY
    for copy in copies:
        copy.wait()
    for g in range(NHEAD):
        cols = slice(g * WIDTH, (g + 1) * WIDTH)
        queries = jnp.concatenate([b0[:, cols].astype(F32), b1[:, cols].astype(F32)], axis=0).astype(BF16)
        fresh = [ref[:, cols].astype(F32) for ref in (b2, b3, b4, b5)]
        for y in range(NY):
            rows = slice(y * share, (y + 1) * share)
            part = jnp.concatenate([f[rows] for f in fresh], axis=0).astype(BF16)
            out[y * NHEAD + g, 0 : 2 * TOK, :] = queries
            out[y * NHEAD + g, 2 * TOK : BLOCK, :] = part


def split3(x):
    hi = x.astype(BF16)
    rest = x - hi.astype(F32)
    mid = rest.astype(BF16)
    lo = (rest - mid.astype(F32)).astype(BF16)
    return hi, mid, lo


def nt_dot(a, b):
    return lax.dot_general(a, b, (((1,), (1,)), ((), ())), preferred_element_type=F32)


def attend_kernel(step_ref, recv, own, other, gates, out):
    my_z = lax.axis_index("z")
    my_y = lax.axis_index("y")
    keys = NZ * PATCH
    rows = 2 * PATCH
    fresh_rows = NHEAD * 2 * FRESH
    col = lax.broadcasted_iota(jnp.int32, (1, keys), 1)
    own_bias = jnp.where(col // PATCH == my_z, NEG, 0.0)
    q_step = (lax.broadcasted_iota(jnp.int32, (rows, fresh_rows), 0) // TOK) % 2
    f_kind = lax.broadcasted_iota(jnp.int32, (rows, fresh_rows), 1) % (2 * FRESH) // (FRESH // 2)
    fresh_bias = jnp.where(f_kind == q_step, 0.0, NEG)
    at = lax.broadcasted_iota(jnp.int32, (fresh_rows, fresh_rows), 0)
    to = lax.broadcasted_iota(jnp.int32, (fresh_rows, fresh_rows), 1)
    shift = jnp.where(to == at + FRESH, 1.0, 0.0).astype(BF16)
    gate0 = gates[pl.ds(step_ref[0], 1), :]
    gate1 = gates[pl.ds(step_ref[1], 1), :]
    lane = lax.broadcasted_iota(jnp.int32, (rows, HDIM), 1)
    step_of_row = (lax.broadcasted_iota(jnp.int32, (rows, HDIM), 0) // TOK) % 2
    slot = lane - 3 * GROUP * step_of_row
    stats = [jnp.zeros((rows, HDIM), F32) for _ in range(NY)]
    for head in range(GROUP):
        cols = slice(head * HDIM, (head + 1) * HDIM)
        vcols = slice(WIDTH + head * HDIM, WIDTH + (head + 1) * HDIM)
        q = recv[:, 0 : 2 * TOK, cols].reshape(NY * rows, HDIM)
        s_own = nt_dot(q, own[:, cols])
        s_other = nt_dot(q, other[:, cols])
        w_own, w_other, tops, totals, accs = [], [], [], [], []
        for y in range(NY):
            part = slice(y * rows, (y + 1) * rows)
            fresh = recv[y * NHEAD : (y + 1) * NHEAD, 2 * TOK : BLOCK, cols].astype(F32)
            fresh = fresh.reshape(fresh_rows, HDIM).astype(BF16)
            fresh_v = jnp.dot(shift, fresh, preferred_element_type=F32).astype(BF16)
            s_f = nt_dot(q[part], fresh) + fresh_bias
            s_a = s_own[part] + jnp.where(my_y == y, own_bias, 0.0)
            s_b = s_other[part]
            top = jnp.maximum(
                jnp.max(jnp.maximum(s_a, s_b), axis=1, keepdims=True), jnp.max(s_f, axis=1, keepdims=True)
            )
            p_a = jnp.exp2((s_a - top) * SCALE2)
            p_b = jnp.exp2((s_b - top) * SCALE2)
            p_f = jnp.exp2((s_f - top) * SCALE2)
            totals.append(jnp.sum(p_a + p_b, axis=1, keepdims=True) + jnp.sum(p_f, axis=1, keepdims=True))
            tops.append(top)
            w_own.append(p_a.astype(BF16))
            w_other.append(p_b.astype(BF16))
            accs.append(jnp.dot(p_f.astype(BF16), fresh_v, preferred_element_type=F32))
        acc = jnp.dot(jnp.concatenate(w_own, axis=0), own[:, vcols], preferred_element_type=F32)
        acc = acc + jnp.dot(jnp.concatenate(w_other, axis=0), other[:, vcols], preferred_element_type=F32)
        gate = jnp.where(step_of_row == 0, gate0[:, cols], gate1[:, cols])
        for y in range(NY):
            mixed = ((acc[y * rows : (y + 1) * rows] + accs[y]) / totals[y]) * gate
            out[y * NHEAD : (y + 1) * NHEAD, head * 2 * TOK : (head + 1) * 2 * TOK, :] = (
                mixed.astype(BF16).reshape(NHEAD, 2 * TOK, HDIM)
            )
            size = tops[y] * SCALE2 + jnp.log(totals[y]) * (1.0 / LN2)
            for i, piece in enumerate(split3(size)):
                stats[y] = jnp.where(slot == 3 * head + i, piece.astype(F32), stats[y])
    for y in range(NY):
        folded = jnp.sum(stats[y].reshape(NHEAD, 2, TOK, HDIM), axis=1)
        out[y * NHEAD : (y + 1) * NHEAD, SENT - TOK : SENT, :] = folded.astype(BF16)


def merge_kernel(recv, out_first, out_second):
    at = lax.broadcasted_iota(jnp.int32, (HDIM, 2 * WIDTH), 0)
    to = lax.broadcasted_iota(jnp.int32, (HDIM, 2 * WIDTH), 1)
    spread = jnp.where(at // 3 == to // HDIM, 1.0, 0.0).astype(BF16)
    sizes, parts = [], []
    for y in range(NY):
        blocks = slice(y * NHEAD, (y + 1) * NHEAD)
        stats = recv[blocks, SENT - TOK : SENT, :].astype(F32).reshape(NHEAD * TOK, HDIM).astype(BF16)
        sizes.append(jnp.dot(stats, spread, preferred_element_type=F32))
        parts.append(recv[blocks, 0 : SENT - TOK, :].astype(F32))
    for step, out in ((0, out_first), (1, out_second)):
        for head in range(GROUP):
            lanes = slice((step * GROUP + head) * HDIM, (step * GROUP + head + 1) * HDIM)
            rows = slice((2 * head + step) * TOK, (2 * head + step + 1) * TOK)
            size = [s[:, lanes] for s in sizes]
            top = functools.reduce(jnp.maximum, size)
            total = jnp.zeros_like(top)
            acc = jnp.zeros_like(top)
            for y in range(NY):
                weight = jnp.exp2(size[y] - top)
                total = total + weight
                acc = acc + weight * parts[y][:, rows, :].reshape(NHEAD * TOK, HDIM)
            result = (acc / total).astype(BF16)
            for g in range(NHEAD):
                cols = slice(g * WIDTH + head * HDIM, g * WIDTH + (head + 1) * HDIM)
                out[:, cols] = result[g * TOK : (g + 1) * TOK]


def vmem(n):
    return [pl.BlockSpec(memory_space=pltpu.VMEM)] * n


def smem(n):
    return [pl.BlockSpec(memory_space=pltpu.SMEM)] * n


PARAMS = pltpu.CompilerParams(vmem_limit_bytes=40 * 1024 * 1024)
PACK_PARAMS = pltpu.CompilerParams(vmem_limit_bytes=62 * 1024 * 1024)


def body(q1, k1, v1, q2, k2, v2, key_stale, value_stale, gate_table, step_index):
    shape = jax.ShapeDtypeStruct
    packed, kv = pl.pallas_call(
        pack_kernel,
        out_shape=(shape((PEERS, BLOCK, WIDTH), BF16), shape((PATCH, 2 * WIDTH), BF16)),
        in_specs=[pl.BlockSpec(memory_space=pltpu.HBM)] * 8,
        out_specs=tuple(vmem(2)),
        scratch_shapes=[pltpu.VMEM((TOK, NHEAD * WIDTH), BF16)] * 6 + [pltpu.SemaphoreType.DMA((8,))],
        compiler_params=PACK_PARAMS,
        name="pack",
    )(q1, k1, v1, q2, k2, v2, key_stale, value_stale)
    recv = lax.all_to_all(packed, PLANE, split_axis=0, concat_axis=0, tiled=True)
    own = lax.all_gather(kv, "z", axis=0, tiled=True)
    other = lax.ppermute(own, "c", [(0, 1), (1, 0)])
    partial = pl.pallas_call(
        attend_kernel,
        out_shape=shape((PEERS, SENT, HDIM), BF16),
        in_specs=smem(1) + vmem(4),
        out_specs=vmem(1)[0],
        compiler_params=PARAMS,
        name="attend",
    )(step_index, recv, own, other, gate_table)
    back = lax.all_to_all(partial, PLANE, split_axis=0, concat_axis=0, tiled=True)
    return pl.pallas_call(
        merge_kernel,
        out_shape=(shape((TOK, NHEAD * WIDTH), BF16),) * 2,
        in_specs=vmem(1),
        out_specs=tuple(vmem(2)),
        compiler_params=PARAMS,
        name="merge",
    )(back)


def solution(mesh):
    fine = Mesh(mesh.devices.reshape(NZ, NY, NC, NH, NX), ("z", "y", "c", "h", "x"))
    tokens = P(("z", "y", "c", "h", "x"), None)
    kept = P(("z", "y", "c"), ("h", "x"))
    return jax.shard_map(
        body,
        mesh=fine,
        in_specs=(tokens,) * 6 + (kept, kept, P(None, ("h", "x")), P()),
        out_specs=(tokens, tokens),
        check_vma=False,
    )
```

time: 90.9 us -> 83.8 us (0.922)
  local copies, waits for them, and re-layouts: 6.39 us -> 0.02 us
  blocking collectives: 54.7 us -> 53 us
    unnamed x20 -> x6, local copies, waits for them, and re-layouts: 6.39 us -> 0.02 us
    all_to_all x1, blocking collectives: 26.7 us -> 25 us  [body(): lax.all_to_all(partial, PLANE, split_axis=0, concat_axis=0, tiled=True)]
    pallas_call x1, Pallas kernels: 0.93 us -> 1.96 us  [body(): pl.pallas_call(pack_kernel, out_shape=(shape((PEERS, BLOCK, WIDTH), BF16)...]
where the time goes in v2:
time: 83.8 us; the launch traced here: 82.5 us
  blocking collectives  53 us (63%)
  starting transfers between devices  18.1 us (22%)
  Pallas kernels  8.81 us (11%)
  waiting for transfers between devices  1.89 us (2%)
    all_gather x1, blocking collectives, body(): own = lax.all_gather(kv, 'z', axis=0, tiled=True)  28 us
    all_to_all x1, blocking collectives, body(): lax.all_to_all(partial, PLANE, split_axis=0, concat_axis=0, tiled=True)  25 us
    all_to_all x1, starting transfers between devices, body(): lax.all_to_all(packed, PLANE, split_axis=0, concat_axis=0, tiled=True)  10.6 us
    ppermute x1, starting transfers between devices, body(): other = lax.ppermute(own, 'c', [(0, 1), (1, 0)])  7.44 us
    pallas_call x1, Pallas kernels, body(): pl.pallas_call(attend_kernel, out_shape=shape((PEERS, SENT, HDIM), BF16),...  5.79 us
    pallas_call x1, Pallas kernels, body(): pl.pallas_call(pack_kernel, out_shape=(shape((PEERS, BLOCK, WIDTH), BF16)...  1.96 us
    ppermute x1, waiting for transfers between devices, body(): other = lax.ppermute(own, 'c', [(0, 1), (1, 0)])  1.89 us
  transfers between devices with their start and end apart: 2, of which 1 were waited for; matrix products, arithmetic and copies ran while one was open for 0% of the time, Pallas kernels for 0%

profile of v2, /device:TPU:1, one launch (start us, length us, event | category | flops | bytes accessed | tf_op | source)
XLA Modules:
  0.0 82.5 jit_solution(1426649843691317556)
XLA Ops:
  0.6 2.0 %pack.1 = (bf16[32,24,384]{2,1,0:T(8,128)(2,1)}, bf16[64,768]{1,0:T(8,128)(2,1)}) custom-call(bf16[8,3072]{1,0:T(8,128)(2,1)} %q1.1, bf16[8,3072]{1,0:T(8,128)(2,1)} %k1.1, bf16[8,3072]{1,0:T(8,128)(2,1)} %v1.1, bf16[8,3072]{1,0:T(8,128)(2,1)} %q2.1, bf16[8,3072]{1,0:T(8,128)(2,1)} %k2.1, bf16[8,3072]{1,0:T(8,128)(2,1)} %v2.1, bf16[64,384]{1,0:T(8,128)(2,1)} %ks.1, ...), custom_call_target="tpu_custom_call" | custom-call | tf_op jit(solution)/shard_map/pack/pallas_call | solution.py:166
  2.6 0.0 copy-start.2
  2.6 10.6 %all-to-all-start = ((bf16[32,24,384]{2,1,0:T(8,128)(2,1)}), bf16[32,24,384]{2,1,0:T(8,128)(2,1)S(1)}, u32[]{:S(2)}, u32[]{:S(2)}) async-start(bf16[32,24,384]{2,1,0:T(8,128)(2,1)} %get-tuple-element.4), calls=%async_computation | async-start | bytes 1179648 | tf_op jit(solution)/shard_map/all_to_all | solution.py:175
  13.3 0.0 copy-done.2
  13.3 0.0 copy-start
  13.3 0.0 copy-start.1
  13.3 28.0 %all_gather.3.own = bf16[512,768]{1,0:T(8,128)(2,1)S(1)} all-gather(bf16[64,768]{1,0:T(8,128)(2,1)S(1)} %copy-done.2), channel_id=1, replica_groups=mesh['z'=8,'y'=4,'c'=2,'h'=2,'x'=4] {'z'}, dimensions={0}, use_global_device_ids=true | all-gather | bytes 884736 | tf_op jit(solution)/shard_map/all_gather | solution.py:176
  41.3 7.4 %collective-permute-start = (bf16[512,768]{1,0:T(8,128)(2,1)S(1)}, bf16[512,768]{1,0:T(8,128)(2,1)S(1)}, u32[]{:S(2)}, u32[]{:S(2)}) collective-permute-start(bf16[512,768]{1,0:T(8,128)(2,1)S(1)} %all_gather.3.own), channel_id=1, source_target_pairs={{0,8},{8,0},{1,9},{9,1},{2,10},{10,2},{3,11},{11,3},{4,12},{12,4},... | collective-permute-start | bytes 2359304 | tf_op jit(solution)/shard_map/ppermute | solution.py:177
  48.7 1.9 %collective-permute-done.other = bf16[512,768]{1,0:T(8,128)(2,1)S(1)} collective-permute-done((bf16[512,768]{1,0:T(8,128)(2,1)S(1)}, bf16[512,768]{1,0:T(8,128)(2,1)S(1)}, u32[]{:S(2)}, u32[]{:S(2)}) %collective-permute-start) | collective-permute-done | bytes 786464 | tf_op jit(solution)/shard_map/ppermute | solution.py:177
  50.6 0.0 all-to-all-done.recv
  50.6 0.0 copy-done
  50.6 0.0 copy-done.1
  50.6 5.8 %attend.1 = bf16[32,56,128]{2,1,0:T(8,128)(2,1)S(1)} custom-call(s32[2]{0:T(128)S(1)} %copy-done.1, bf16[32,24,384]{2,1,0:T(8,128)(2,1)S(1)} %all-to-all-done.recv, bf16[512,768]{1,0:T(8,128)(2,1)S(1)} %all_gather.3.own, bf16[512,768]{1,0:T(8,128)(2,1)S(1)} %collective-permute-done.other, f32[50,384]{1,0:T(8,128)S(1)} %copy-done), custom_call_target="tpu_custom_call" | custom-call | tf_op jit(solution)/shard_map/attend/pallas_call | solution.py:178
  56.4 25.0 %all_to_all.10.recv = bf16[32,56,128]{2,1,0:T(8,128)(2,1)S(1)} all-to-all(bf16[32,56,128]{2,1,0:T(8,128)(2,1)S(1)} %attend.1), channel_id=1, replica_groups=mesh['z'=8,'y'=4,'c'=2,'h'=2,'x'=4] {'y','h','x'}, dimensions={0} | all-to-all | bytes 917504 | tf_op jit(solution)/shard_map/all_to_all | solution.py:186
  81.5 1.1 %merge.1 = (bf16[8,3072]{1,0:T(8,128)(2,1)}, bf16[8,3072]{1,0:T(8,128)(2,1)}) custom-call(bf16[32,56,128]{2,1,0:T(8,128)(2,1)S(1)} %all_to_all.10.recv), custom_call_target="tpu_custom_call" | custom-call | tf_op jit(solution)/shard_map/merge/pallas_call | solution.py:187
Async XLA Ops:
  2.6 10.7 %copy-start.2 = (bf16[64,768]{1,0:T(8,128)(2,1)S(1)}, bf16[64,768]{1,0:T(8,128)(2,1)}, u32[]{:S(2)}) copy-start(bf16[64,768]{1,0:T(8,128)(2,1)} %get-tuple-element.5) | copy-start | bytes 294916
  2.6 48.0 %all-to-all-start = ((bf16[32,24,384]{2,1,0:T(8,128)(2,1)}), bf16[32,24,384]{2,1,0:T(8,128)(2,1)S(1)}, u32[]{:S(2)}, u32[]{:S(2)}) async-start(bf16[32,24,384]{2,1,0:T(8,128)(2,1)} %get-tuple-element.4), calls=%async_computation | async-start | bytes 1179648 | tf_op jit(solution)/shard_map/all_to_all | solution.py:175
  13.3 37.4 %copy-start = (f32[50,384]{1,0:T(8,128)S(1)}, f32[50,384]{1,0:T(8,128)}, u32[]{:S(2)}) copy-start(f32[50,384]{1,0:T(8,128)} %gates.1) | copy-start | bytes 230404
  13.3 37.4 %copy-start.1 = (s32[2]{0:T(128)S(1)}, s32[2]{0:T(128)}, u32[]{:S(2)}) copy-start(s32[2]{0:T(128)} %step_ref.1) | copy-start | bytes 28
  41.3 9.3 %collective-permute-start = (bf16[512,768]{1,0:T(8,128)(2,1)S(1)}, bf16[512,768]{1,0:T(8,128)(2,1)S(1)}, u32[]{:S(2)}, u32[]{:S(2)}) collective-permute-start(bf16[512,768]{1,0:T(8,128)(2,1)S(1)} %all_gather.3.own), channel_id=1, source_target_pairs={{0,8},{8,0},{1,9},{9,1},{2,10},{10,2},{3,11},{11,3},{4,12},{12,4},... | collective-permute-start | bytes 2359304 | tf_op jit(solution)/shard_map/ppermute | solution.py:177

commit v3 on v2

--- a/solution.py
+++ b/solution.py
@@ -60,13 +60,13 @@
 
 
 def attend_kernel(step_ref, recv, own, other, gates, out):
-    my_z = lax.axis_index("z")
+    mine = 2 * lax.axis_index("zq")
     my_y = lax.axis_index("y")
     keys = NZ * PATCH
     rows = 2 * PATCH
     fresh_rows = NHEAD * 2 * FRESH
     col = lax.broadcasted_iota(jnp.int32, (1, keys), 1)
-    own_bias = jnp.where(col // PATCH == my_z, NEG, 0.0)
+    own_bias = jnp.where(col // PATCH == mine, NEG, 0.0)
     q_step = (lax.broadcasted_iota(jnp.int32, (rows, fresh_rows), 0) // TOK) % 2
     f_kind = lax.broadcasted_iota(jnp.int32, (rows, fresh_rows), 1) % (2 * FRESH) // (FRESH // 2)
     fresh_bias = jnp.where(f_kind == q_step, 0.0, NEG)
@@ -79,21 +79,30 @@
     step_of_row = (lax.broadcasted_iota(jnp.int32, (rows, HDIM), 0) // TOK) % 2
     slot = lane - 3 * GROUP * step_of_row
     stats = [jnp.zeros((rows, HDIM), F32) for _ in range(NY)]
-    for head in range(GROUP):
+
+    def scores(head):
         cols = slice(head * HDIM, (head + 1) * HDIM)
-        vcols = slice(WIDTH + head * HDIM, WIDTH + (head + 1) * HDIM)
         q = recv[:, 0 : 2 * TOK, cols].reshape(NY * rows, HDIM)
-        s_own = nt_dot(q, own[:, cols])
-        s_other = nt_dot(q, other[:, cols])
-        w_own, w_other, tops, totals, accs = [], [], [], [], []
-        for y in range(NY):
-            part = slice(y * rows, (y + 1) * rows)
+        extra = []
+        for y in range(NY):
             fresh = recv[y * NHEAD : (y + 1) * NHEAD, 2 * TOK : BLOCK, cols].astype(F32)
             fresh = fresh.reshape(fresh_rows, HDIM).astype(BF16)
             fresh_v = jnp.dot(shift, fresh, preferred_element_type=F32).astype(BF16)
-            s_f = nt_dot(q[part], fresh) + fresh_bias
+            extra.append((nt_dot(q[y * rows : (y + 1) * rows], fresh) + fresh_bias, fresh_v))
+        return nt_dot(q, own[:, cols]), nt_dot(q, other[:, cols]), extra
+
+    ready = scores(0)
+    for head in range(GROUP):
+        vcols = slice(WIDTH + head * HDIM, WIDTH + (head + 1) * HDIM)
+        s_own, s_other, extra = ready
+        if head + 1 < GROUP:
+            ready = scores(head + 1)
+        w_own, w_other, tops, totals, accs = [], [], [], [], []
+        for y in range(NY):
+            part = slice(y * rows, (y + 1) * rows)
             s_a = s_own[part] + jnp.where(my_y == y, own_bias, 0.0)
             s_b = s_other[part]
+            s_f, fresh_v = extra[y]
             top = jnp.maximum(
                 jnp.max(jnp.maximum(s_a, s_b), axis=1, keepdims=True), jnp.max(s_f, axis=1, keepdims=True)
             )
@@ -107,6 +116,7 @@
             accs.append(jnp.dot(p_f.astype(BF16), fresh_v, preferred_element_type=F32))
         acc = jnp.dot(jnp.concatenate(w_own, axis=0), own[:, vcols], preferred_element_type=F32)
         acc = acc + jnp.dot(jnp.concatenate(w_other, axis=0), other[:, vcols], preferred_element_type=F32)
+        cols = slice(head * HDIM, (head + 1) * HDIM)
         gate = jnp.where(step_of_row == 0, gate0[:, cols], gate1[:, cols])
         for y in range(NY):
             mixed = ((acc[y * rows : (y + 1) * rows] + accs[y]) / totals[y]) * gate
@@ -173,7 +183,8 @@
         name="pack",
     )(q1, k1, v1, q2, k2, v2, key_stale, value_stale)
     recv = lax.all_to_all(packed, PLANE, split_axis=0, concat_axis=0, tiled=True)
-    own = lax.all_gather(kv, "z", axis=0, tiled=True)
+    pair = lax.ppermute(kv, "zp", [(0, 1), (1, 0)])
+    own = lax.all_gather(jnp.concatenate([kv, pair], axis=0), "zq", axis=0, tiled=True)
     other = lax.ppermute(own, "c", [(0, 1), (1, 0)])
     partial = pl.pallas_call(
         attend_kernel,
@@ -195,9 +206,9 @@
 
 
 def solution(mesh):
-    fine = Mesh(mesh.devices.reshape(NZ, NY, NC, NH, NX), ("z", "y", "c", "h", "x"))
-    tokens = P(("z", "y", "c", "h", "x"), None)
-    kept = P(("z", "y", "c"), ("h", "x"))
+    fine = Mesh(mesh.devices.reshape(NZ // 2, 2, NY, NC, NH, NX), ("zq", "zp", "y", "c", "h", "x"))
+    tokens = P(("zq", "zp", "y", "c", "h", "x"), None)
+    kept = P(("zq", "zp", "y", "c"), ("h", "x"))
     return jax.shard_map(
         body,
         mesh=fine,

time: 83.8 us -> 77.8 us (0.928)
  blocking collectives: 53 us -> 47.5 us
  Pallas kernels: 8.81 us -> 6.64 us
  starting transfers between devices: 18.1 us -> 19.8 us
    all_gather x1, blocking collectives: 28 us -> 23.2 us  [body(): lax.all_gather(jnp.concatenate([kv, pair], axis=0), 'zq', axis=0, tiled=T...]
    ppermute x0 -> x1, starting transfers between devices: none -> 4.83 us  [body(): pair = lax.ppermute(kv, 'zp', [(0, 1), (1, 0)])]
    ppermute x1, starting transfers between devices: 7.44 us -> 5.13 us  [body(): other = lax.ppermute(own, 'c', [(0, 1), (1, 0)])]
    pallas_call x1, Pallas kernels: 5.79 us -> 3.63 us  [body(): pl.pallas_call(attend_kernel, out_shape=shape((PEERS, SENT, HDIM), BF16),...]
  transfers between devices with their start and end apart: 2 -> 3, of which waited for: 1 -> 1; matrix products, arithmetic and copies ran while one was open for 0% -> 0% of each run, Pallas kernels for 0% -> 0%
where the time goes in v3:
time: 77.8 us; the launch traced here: 76.5 us
  blocking collectives  47.5 us (61%)
  starting transfers between devices  19.8 us (25%)
  Pallas kernels  6.64 us (9%)
  waiting for transfers between devices  1.9 us (2%)
    all_to_all x1, blocking collectives, body(): lax.all_to_all(partial, PLANE, split_axis=0, concat_axis=0, tiled=True)  24.3 us
    all_gather x1, blocking collectives, body(): lax.all_gather(jnp.concatenate([kv, pair], axis=0), 'zq', axis=0, tiled=T...  23.2 us
    all_to_all x1, starting transfers between devices, body(): lax.all_to_all(packed, PLANE, split_axis=0, concat_axis=0, tiled=True)  9.81 us
    ppermute x1, starting transfers between devices, body(): other = lax.ppermute(own, 'c', [(0, 1), (1, 0)])  5.13 us
    ppermute x1, starting transfers between devices, body(): pair = lax.ppermute(kv, 'zp', [(0, 1), (1, 0)])  4.83 us
    pallas_call x1, Pallas kernels, body(): pl.pallas_call(attend_kernel, out_shape=shape((PEERS, SENT, HDIM), BF16),...  3.63 us
    pallas_call x1, Pallas kernels, body(): pl.pallas_call(pack_kernel, out_shape=(shape((PEERS, BLOCK, WIDTH), BF16)...  1.95 us
    ppermute x1, waiting for transfers between devices, body(): other = lax.ppermute(own, 'c', [(0, 1), (1, 0)])  1.89 us
  transfers between devices with their start and end apart: 3, of which 1 were waited for; matrix products, arithmetic and copies ran while one was open for 0% of the time, Pallas kernels for 0%

profile of v3, /device:TPU:1, one launch (start us, length us, event | category | flops | bytes accessed | tf_op | source)
XLA Modules:
  0.0 76.5 jit_solution(16882215576366045586)
XLA Ops:
  0.6 2.0 %pack.1 = (bf16[32,24,384]{2,1,0:T(8,128)(2,1)}, bf16[64,768]{1,0:T(8,128)(2,1)}) custom-call(bf16[8,3072]{1,0:T(8,128)(2,1)} %q1.1, bf16[8,3072]{1,0:T(8,128)(2,1)} %k1.1, bf16[8,3072]{1,0:T(8,128)(2,1)} %v1.1, bf16[8,3072]{1,0:T(8,128)(2,1)} %q2.1, bf16[8,3072]{1,0:T(8,128)(2,1)} %k2.1, bf16[8,3072]{1,0:T(8,128)(2,1)} %v2.1, bf16[64,384]{1,0:T(8,128)(2,1)} %ks.1, ...), custom_call_target="tpu_custom_call" | custom-call | tf_op jit(solution)/shard_map/pack/pallas_call | solution.py:176
  2.6 4.8 %collective-permute-start = (bf16[64,768]{1,0:T(8,128)(2,1)}, bf16[64,768]{1,0:T(8,128)(2,1)S(1)}, u32[]{:S(2)}, u32[]{:S(2)}) collective-permute-start(bf16[64,768]{1,0:T(8,128)(2,1)} %get-tuple-element.5), channel_id=1, source_target_pairs={{0,64},{64,0},{1,65},{65,1},{2,66},{66,2},{3,67},{67,3},{4,68},{68... | collective-permute-start | bytes 294920 | tf_op jit(solution)/shard_map/ppermute | solution.py:186
  7.4 0.0 copy-start.2
  7.4 9.8 %all-to-all-start = ((bf16[32,24,384]{2,1,0:T(8,128)(2,1)}), bf16[32,24,384]{2,1,0:T(8,128)(2,1)S(1)}, u32[]{:S(2)}, u32[]{:S(2)}) async-start(bf16[32,24,384]{2,1,0:T(8,128)(2,1)} %get-tuple-element.4), calls=%async_computation | async-start | bytes 1179648 | tf_op jit(solution)/shard_map/all_to_all | solution.py:185
  17.3 0.0 collective-permute-done
  17.3 0.0 copy-done.2
  17.3 0.0 copy-start
  17.3 0.0 copy-start.1
  17.3 23.2 %all_gather.3.own = bf16[512,768]{1,0:T(8,128)(2,1)S(1)} all-gather(bf16[128,768]{1,0:T(8,128)(2,1)S(1)} %pad_maximum_fusion), channel_id=1, replica_groups=mesh['zq'=4,'zp'=2,'y'=4,'c'=2,'h'=2,'x'=4] {'zq'}, dimensions={0}, use_global_device_ids=true | all-gather | bytes 983040 | tf_op jit(solution)/shard_map/all_gather | solution.py:187
  40.5 5.1 %collective-permute-start.1 = (bf16[512,768]{1,0:T(8,128)(2,1)S(1)}, bf16[512,768]{1,0:T(8,128)(2,1)S(1)}, u32[]{:S(2)}, u32[]{:S(2)}) collective-permute-start(bf16[512,768]{1,0:T(8,128)(2,1)S(1)} %all_gather.3.own), channel_id=1, source_target_pairs={{0,8},{8,0},{1,9},{9,1},{2,10},{10,2},{3,11},{11,3},{4,12},{12,4},... | collective-permute-start | bytes 2359304 | tf_op jit(solution)/shard_map/ppermute | solution.py:188
  45.6 1.9 %collective-permute-done.1.other = bf16[512,768]{1,0:T(8,128)(2,1)S(1)} collective-permute-done((bf16[512,768]{1,0:T(8,128)(2,1)S(1)}, bf16[512,768]{1,0:T(8,128)(2,1)S(1)}, u32[]{:S(2)}, u32[]{:S(2)}) %collective-permute-start.1) | collective-permute-done | bytes 786464 | tf_op jit(solution)/shard_map/ppermute | solution.py:188
  47.5 0.0 all-to-all-done.recv
  47.5 0.0 copy-done
  47.5 0.0 copy-done.1
  47.5 3.6 %attend.1 = bf16[32,56,128]{2,1,0:T(8,128)(2,1)S(1)} custom-call(s32[2]{0:T(128)S(1)} %copy-done.1, bf16[32,24,384]{2,1,0:T(8,128)(2,1)S(1)} %all-to-all-done.recv, bf16[512,768]{1,0:T(8,128)(2,1)S(1)} %all_gather.3.own, bf16[512,768]{1,0:T(8,128)(2,1)S(1)} %collective-permute-done.1.other, f32[50,384]{1,0:T(8,128)S(1)} %copy-done), custom_call_target="tpu_custom_call" | custom-call | tf_op jit(solution)/shard_map/attend/pallas_call | solution.py:189
  51.1 24.3 %all_to_all.10.recv = bf16[32,56,128]{2,1,0:T(8,128)(2,1)S(1)} all-to-all(bf16[32,56,128]{2,1,0:T(8,128)(2,1)S(1)} %attend.1), channel_id=1, replica_groups=mesh['zq'=4,'zp'=2,'y'=4,'c'=2,'h'=2,'x'=4] {'y','h','x'}, dimensions={0} | all-to-all | bytes 917504 | tf_op jit(solution)/shard_map/all_to_all | solution.py:197
  75.5 1.1 %merge.1 = (bf16[8,3072]{1,0:T(8,128)(2,1)}, bf16[8,3072]{1,0:T(8,128)(2,1)}) custom-call(bf16[32,56,128]{2,1,0:T(8,128)(2,1)S(1)} %all_to_all.10.recv), custom_call_target="tpu_custom_call" | custom-call | tf_op jit(solution)/shard_map/merge/pallas_call | solution.py:198
  (1 shorter events, 0.0 us)
Async XLA Ops:
  2.6 14.7 %collective-permute-start = (bf16[64,768]{1,0:T(8,128)(2,1)}, bf16[64,768]{1,0:T(8,128)(2,1)S(1)}, u32[]{:S(2)}, u32[]{:S(2)}) collective-permute-start(bf16[64,768]{1,0:T(8,128)(2,1)} %get-tuple-element.5), channel_id=1, source_target_pairs={{0,64},{64,0},{1,65},{65,1},{2,66},{66,2},{3,67},{67,3},{4,68},{68... | collective-permute-start | bytes 294920 | tf_op jit(solution)/shard_map/ppermute | solution.py:186
  7.4 9.8 %copy-start.2 = (bf16[64,768]{1,0:T(8,128)(2,1)S(1)}, bf16[64,768]{1,0:T(8,128)(2,1)}, u32[]{:S(2)}) copy-start(bf16[64,768]{1,0:T(8,128)(2,1)} %get-tuple-element.5) | copy-start | bytes 294916
  7.4 40.1 %all-to-all-start = ((bf16[32,24,384]{2,1,0:T(8,128)(2,1)}), bf16[32,24,384]{2,1,0:T(8,128)(2,1)S(1)}, u32[]{:S(2)}, u32[]{:S(2)}) async-start(bf16[32,24,384]{2,1,0:T(8,128)(2,1)} %get-tuple-element.4), calls=%async_computation | async-start | bytes 1179648 | tf_op jit(solution)/shard_map/all_to_all | solution.py:185
  17.3 30.2 %copy-start = (f32[50,384]{1,0:T(8,128)S(1)}, f32[50,384]{1,0:T(8,128)}, u32[]{:S(2)}) copy-start(f32[50,384]{1,0:T(8,128)} %gates.1) | copy-start | bytes 230404
  17.3 30.2 %copy-start.1 = (s32[2]{0:T(128)S(1)}, s32[2]{0:T(128)}, u32[]{:S(2)}) copy-start(s32[2]{0:T(128)} %step_ref.1) | copy-start | bytes 28
  40.5 7.0 %collective-permute-start.1 = (bf16[512,768]{1,0:T(8,128)(2,1)S(1)}, bf16[512,768]{1,0:T(8,128)(2,1)S(1)}, u32[]{:S(2)}, u32[]{:S(2)}) collective-permute-start(bf16[512,768]{1,0:T(8,128)(2,1)S(1)} %all_gather.3.own), channel_id=1, source_target_pairs={{0,8},{8,0},{1,9},{9,1},{2,10},{10,2},{3,11},{11,3},{4,12},{12,4},... | collective-permute-start | bytes 2359304 | tf_op jit(solution)/shard_map/ppermute | solution.py:188

commit v4 on v3

--- a/solution.py
+++ b/solution.py
@@ -59,67 +59,113 @@
     return lax.dot_general(a, b, (((1,), (1,)), ((), ())), preferred_element_type=F32)
 
 
-def attend_kernel(step_ref, recv, own, other, gates, out):
+ROWS = 2 * PATCH
+ALL = NY * ROWS
+FRESH_ROWS = NHEAD * 2 * FRESH
+KEYS = NZ * PATCH
+
+
+def head_cols(head):
+    return slice(head * HDIM, (head + 1) * HDIM)
+
+
+def value_cols(head):
+    return slice(WIDTH + head * HDIM, WIDTH + (head + 1) * HDIM)
+
+
+def queries_of(recv, head):
+    return recv[:, 0 : 2 * TOK, head_cols(head)].reshape(ALL, HDIM)
+
+
+def patch_rows(y):
+    return slice(y * ROWS, (y + 1) * ROWS)
+
+
+def row_max(x):
+    return jnp.max(x, axis=1, keepdims=True)
+
+
+def row_sum(x):
+    return jnp.sum(x, axis=1, keepdims=True)
+
+
+def attend_own_kernel(step_ref, recv, own, gates, acc_out, top_out, total_out, gate_out):
     mine = 2 * lax.axis_index("zq")
     my_y = lax.axis_index("y")
-    keys = NZ * PATCH
-    rows = 2 * PATCH
-    fresh_rows = NHEAD * 2 * FRESH
-    col = lax.broadcasted_iota(jnp.int32, (1, keys), 1)
+    col = lax.broadcasted_iota(jnp.int32, (1, KEYS), 1)
     own_bias = jnp.where(col // PATCH == mine, NEG, 0.0)
-    q_step = (lax.broadcasted_iota(jnp.int32, (rows, fresh_rows), 0) // TOK) % 2
-    f_kind = lax.broadcasted_iota(jnp.int32, (rows, fresh_rows), 1) % (2 * FRESH) // (FRESH // 2)
+    q_step = (lax.broadcasted_iota(jnp.int32, (ROWS, FRESH_ROWS), 0) // TOK) % 2
+    f_kind = lax.broadcasted_iota(jnp.int32, (ROWS, FRESH_ROWS), 1) % (2 * FRESH) // (FRESH // 2)
     fresh_bias = jnp.where(f_kind == q_step, 0.0, NEG)
-    at = lax.broadcasted_iota(jnp.int32, (fresh_rows, fresh_rows), 0)
-    to = lax.broadcasted_iota(jnp.int32, (fresh_rows, fresh_rows), 1)
+    at = lax.broadcasted_iota(jnp.int32, (FRESH_ROWS, FRESH_ROWS), 0)
+    to = lax.broadcasted_iota(jnp.int32, (FRESH_ROWS, FRESH_ROWS), 1)
     shift = jnp.where(to == at + FRESH, 1.0, 0.0).astype(BF16)
-    gate0 = gates[pl.ds(step_ref[0], 1), :]
-    gate1 = gates[pl.ds(step_ref[1], 1), :]
-    lane = lax.broadcasted_iota(jnp.int32, (rows, HDIM), 1)
-    step_of_row = (lax.broadcasted_iota(jnp.int32, (rows, HDIM), 0) // TOK) % 2
-    slot = lane - 3 * GROUP * step_of_row
-    stats = [jnp.zeros((rows, HDIM), F32) for _ in range(NY)]
+    for step in range(2):
+        gate = gates[pl.ds(step_ref[step], 1), :]
+        gate_out[step * TOK : (step + 1) * TOK, :] = jnp.broadcast_to(gate, (TOK, WIDTH))
 
     def scores(head):
-        cols = slice(head * HDIM, (head + 1) * HDIM)
-        q = recv[:, 0 : 2 * TOK, cols].reshape(NY * rows, HDIM)
+        q = queries_of(recv, head)
         extra = []
         for y in range(NY):
-            fresh = recv[y * NHEAD : (y + 1) * NHEAD, 2 * TOK : BLOCK, cols].astype(F32)
-            fresh = fresh.reshape(fresh_rows, HDIM).astype(BF16)
+            fresh = recv[y * NHEAD : (y + 1) * NHEAD, 2 * TOK : BLOCK, head_cols(head)].astype(F32)
+            fresh = fresh.reshape(FRESH_ROWS, HDIM).astype(BF16)
             fresh_v = jnp.dot(shift, fresh, preferred_element_type=F32).astype(BF16)
-            extra.append((nt_dot(q[y * rows : (y + 1) * rows], fresh) + fresh_bias, fresh_v))
-        return nt_dot(q, own[:, cols]), nt_dot(q, other[:, cols]), extra
+            extra.append((nt_dot(q[patch_rows(y)], fresh) + fresh_bias, fresh_v))
+        return nt_dot(q, own[:, head_cols(head)]), extra
 
     ready = scores(0)
     for head in range(GROUP):
-        vcols = slice(WIDTH + head * HDIM, WIDTH + (head + 1) * HDIM)
-        s_own, s_other, extra = ready
+        s_own, extra = ready
         if head + 1 < GROUP:
             ready = scores(head + 1)
-        w_own, w_other, tops, totals, accs = [], [], [], [], []
-        for y in range(NY):
-            part = slice(y * rows, (y + 1) * rows)
-            s_a = s_own[part] + jnp.where(my_y == y, own_bias, 0.0)
-            s_b = s_other[part]
+        weights, accs = [], []
+        for y in range(NY):
+            s_a = s_own[patch_rows(y)] + jnp.where(my_y == y, own_bias, 0.0)
             s_f, fresh_v = extra[y]
-            top = jnp.maximum(
-                jnp.max(jnp.maximum(s_a, s_b), axis=1, keepdims=True), jnp.max(s_f, axis=1, keepdims=True)
-            )
+            top = jnp.maximum(row_max(s_a), row_max(s_f))
             p_a = jnp.exp2((s_a - top) * SCALE2)
-            p_b = jnp.exp2((s_b - top) * SCALE2)
             p_f = jnp.exp2((s_f - top) * SCALE2)
-            totals.append(jnp.sum(p_a + p_b, axis=1, keepdims=True) + jnp.sum(p_f, axis=1, keepdims=True))
+            total = row_sum(p_a) + row_sum(p_f)
+            weights.append(p_a.astype(BF16))
+            accs.append(jnp.dot(p_f.astype(BF16), fresh_v, preferred_element_type=F32))
+            top_out[patch_rows(y), head_cols(head)] = jnp.broadcast_to(top, (ROWS, HDIM))
+            total_out[patch_rows(y), head_cols(head)] = jnp.broadcast_to(total, (ROWS, HDIM))
+        acc = jnp.dot(jnp.concatenate(weights, axis=0), own[:, value_cols(head)], preferred_element_type=F32)
+        acc_out[:, head_cols(head)] = acc + jnp.concatenate(accs, axis=0)
+
+
+def attend_other_kernel(recv, other, acc_in, top_in, total_in, gate_in, out):
+    lane = lax.broadcasted_iota(jnp.int32, (ROWS, HDIM), 1)
+    step_of_row = (lax.broadcasted_iota(jnp.int32, (ROWS, HDIM), 0) // TOK) % 2
+    slot = lane - 3 * GROUP * step_of_row
+    stats = [jnp.zeros((ROWS, HDIM), F32) for _ in range(NY)]
+
+    def scores(head):
+        return nt_dot(queries_of(recv, head), other[:, head_cols(head)])
+
+    ready = scores(0)
+    for head in range(GROUP):
+        s_all = ready
+        if head + 1 < GROUP:
+            ready = scores(head + 1)
+        weights, tops, totals, keeps = [], [], [], []
+        for y in range(NY):
+            s_b = s_all[patch_rows(y)]
+            old_top = top_in[patch_rows(y), head_cols(head)]
+            top = jnp.maximum(jnp.broadcast_to(row_max(s_b), (ROWS, HDIM)), old_top)
+            p_b = jnp.exp2((s_b - jnp.concatenate([top] * (KEYS // HDIM), axis=1)) * SCALE2)
+            keep = jnp.exp2((old_top - top) * SCALE2)
             tops.append(top)
-            w_own.append(p_a.astype(BF16))
-            w_other.append(p_b.astype(BF16))
-            accs.append(jnp.dot(p_f.astype(BF16), fresh_v, preferred_element_type=F32))
-        acc = jnp.dot(jnp.concatenate(w_own, axis=0), own[:, vcols], preferred_element_type=F32)
-        acc = acc + jnp.dot(jnp.concatenate(w_other, axis=0), other[:, vcols], preferred_element_type=F32)
-        cols = slice(head * HDIM, (head + 1) * HDIM)
-        gate = jnp.where(step_of_row == 0, gate0[:, cols], gate1[:, cols])
-        for y in range(NY):
-            mixed = ((acc[y * rows : (y + 1) * rows] + accs[y]) / totals[y]) * gate
+            keeps.append(keep)
+            totals.append(jnp.broadcast_to(row_sum(p_b), (ROWS, HDIM)) + keep * total_in[patch_rows(y), head_cols(head)])
+            weights.append(p_b.astype(BF16))
+        acc = jnp.dot(jnp.concatenate(weights, axis=0), other[:, value_cols(head)], preferred_element_type=F32)
+        cols = head_cols(head)
+        gate = jnp.concatenate([gate_in[:, cols]] * NHEAD, axis=0)
+        for y in range(NY):
+            total = acc[patch_rows(y)] + keeps[y] * acc_in[patch_rows(y), cols]
+            mixed = (total / totals[y]) * gate
             out[y * NHEAD : (y + 1) * NHEAD, head * 2 * TOK : (head + 1) * 2 * TOK, :] = (
                 mixed.astype(BF16).reshape(NHEAD, 2 * TOK, HDIM)
             )
@@ -186,14 +232,26 @@
     pair = lax.ppermute(kv, "zp", [(0, 1), (1, 0)])
     own = lax.all_gather(jnp.concatenate([kv, pair], axis=0), "zq", axis=0, tiled=True)
     other = lax.ppermute(own, "c", [(0, 1), (1, 0)])
+    cost = pl.CostEstimate(flops=4 * ALL * KEYS * WIDTH, bytes_accessed=2 << 20, transcendentals=GROUP * ALL * KEYS)
+    state = (shape((ALL, WIDTH), F32),) * 3 + (shape((2 * TOK, WIDTH), F32),)
+    state = pl.pallas_call(
+        attend_own_kernel,
+        out_shape=state,
+        in_specs=smem(1) + vmem(3),
+        out_specs=tuple(vmem(4)),
+        compiler_params=PARAMS,
+        cost_estimate=cost,
+        name="attend_own",
+    )(step_index, recv, own, gate_table)
     partial = pl.pallas_call(
-        attend_kernel,
+        attend_other_kernel,
         out_shape=shape((PEERS, SENT, HDIM), BF16),
-        in_specs=smem(1) + vmem(4),
+        in_specs=vmem(6),
         out_specs=vmem(1)[0],
         compiler_params=PARAMS,
-        name="attend",
-    )(step_index, recv, own, other, gate_table)
+        cost_estimate=cost,
+        name="attend_other",
+    )(recv, other, *state)
     back = lax.all_to_all(partial, PLANE, split_axis=0, concat_axis=0, tiled=True)
     return pl.pallas_call(
         merge_kernel,

time: 77.8 us -> 76.1 us (0.978); the launches traced: 76.5 us -> 75.7 us
  waiting for transfers between devices: 1.9 us -> 0.01 us
  blocking collectives: 47.5 us -> 48.4 us
    ppermute x1, waiting for transfers between devices: 1.89 us -> 0.01 us  [body(): other = lax.ppermute(own, 'c', [(0, 1), (1, 0)])]
    all_to_all x1, blocking collectives: 24.3 us -> 25.2 us  [body(): lax.all_to_all(partial, PLANE, split_axis=0, concat_axis=0, tiled=True)]
    pallas_call x1 -> x2, Pallas kernels: 3.63 us -> 3.78 us  [the longest x1 2.16 us: body(): pl.pallas_call(attend_own_kernel, out_shape=state, in_specs=smem(1) + vme...]
  transfers between devices with their start and end apart: 3 -> 3, of which waited for: 1 -> 0; matrix products, arithmetic and copies ran while one was open for 0% -> 0% of each run, Pallas kernels for 0% -> 3%
where the time goes in v4:
time: 76.1 us; the launch traced here: 75.7 us
  blocking collectives  48.4 us (64%)
  starting transfers between devices  19.8 us (26%)
  Pallas kernels  6.8 us (9%)
    all_to_all x1, blocking collectives, body(): lax.all_to_all(partial, PLANE, split_axis=0, concat_axis=0, tiled=True)  25.2 us
    all_gather x1, blocking collectives, body(): lax.all_gather(jnp.concatenate([kv, pair], axis=0), 'zq', axis=0, tiled=T...  23.2 us
    all_to_all x1, starting transfers between devices, body(): lax.all_to_all(packed, PLANE, split_axis=0, concat_axis=0, tiled=True)  9.81 us
    ppermute x1, starting transfers between devices, body(): other = lax.ppermute(own, 'c', [(0, 1), (1, 0)])  5.13 us
    ppermute x1, starting transfers between devices, body(): pair = lax.ppermute(kv, 'zp', [(0, 1), (1, 0)])  4.83 us
    pallas_call x1, Pallas kernels, body(): pl.pallas_call(attend_own_kernel, out_shape=state, in_specs=smem(1) + vme...  2.16 us
    pallas_call x1, Pallas kernels, body(): pl.pallas_call(pack_kernel, out_shape=(shape((PEERS, BLOCK, WIDTH), BF16)...  1.96 us
    pallas_call x1, Pallas kernels, body(): pl.pallas_call(attend_other_kernel, out_shape=shape((PEERS, SENT, HDIM),...  1.62 us
  transfers between devices with their start and end apart: 3, of which 0 were waited for; matrix products, arithmetic and copies ran while one was open for 0% of the time, Pallas kernels for 3%

profile of v4, /device:TPU:1, one launch (start us, length us, event | category | flops | bytes accessed | tf_op | source)
XLA Modules:
  0.0 75.7 jit_solution(5108167042035770542)
XLA Ops:
  0.6 2.0 %pack.1 = (bf16[32,24,384]{2,1,0:T(8,128)(2,1)}, bf16[64,768]{1,0:T(8,128)(2,1)}) custom-call(bf16[8,3072]{1,0:T(8,128)(2,1)} %q1.1, bf16[8,3072]{1,0:T(8,128)(2,1)} %k1.1, bf16[8,3072]{1,0:T(8,128)(2,1)} %v1.1, bf16[8,3072]{1,0:T(8,128)(2,1)} %q2.1, bf16[8,3072]{1,0:T(8,128)(2,1)} %k2.1, bf16[8,3072]{1,0:T(8,128)(2,1)} %v2.1, bf16[64,384]{1,0:T(8,128)(2,1)} %ks.1, ...), custom_call_target="tpu_custom_call" | custom-call | tf_op jit(solution)/shard_map/pack/pallas_call | solution.py:222
  2.6 4.8 %collective-permute-start = (bf16[64,768]{1,0:T(8,128)(2,1)}, bf16[64,768]{1,0:T(8,128)(2,1)S(1)}, u32[]{:S(2)}, u32[]{:S(2)}) collective-permute-start(bf16[64,768]{1,0:T(8,128)(2,1)} %get-tuple-element.9), channel_id=1, source_target_pairs={{0,64},{64,0},{1,65},{65,1},{2,66},{66,2},{3,67},{67,3},{4,68},{68... | collective-permute-start | bytes 294920 | tf_op jit(solution)/shard_map/ppermute | solution.py:232
  7.4 0.0 copy-start.2
  7.5 9.8 %all-to-all-start = ((bf16[32,24,384]{2,1,0:T(8,128)(2,1)}), bf16[32,24,384]{2,1,0:T(8,128)(2,1)S(1)}, u32[]{:S(2)}, u32[]{:S(2)}) async-start(bf16[32,24,384]{2,1,0:T(8,128)(2,1)} %get-tuple-element.8), calls=%async_computation | async-start | bytes 1179648 | tf_op jit(solution)/shard_map/all_to_all | solution.py:231
  17.3 0.0 collective-permute-done
  17.3 0.0 copy-done.2
  17.3 0.0 copy-start
  17.3 0.0 copy-start.1
  17.3 23.2 %all_gather.3.own = bf16[512,768]{1,0:T(8,128)(2,1)S(1)} all-gather(bf16[128,768]{1,0:T(8,128)(2,1)S(1)} %pad_maximum_fusion), channel_id=1, replica_groups=mesh['zq'=4,'zp'=2,'y'=4,'c'=2,'h'=2,'x'=4] {'zq'}, dimensions={0}, use_global_device_ids=true | all-gather | bytes 983040 | tf_op jit(solution)/shard_map/all_gather | solution.py:233
  40.5 5.1 %collective-permute-start.1 = (bf16[512,768]{1,0:T(8,128)(2,1)S(1)}, bf16[512,768]{1,0:T(8,128)(2,1)S(1)}, u32[]{:S(2)}, u32[]{:S(2)}) collective-permute-start(bf16[512,768]{1,0:T(8,128)(2,1)S(1)} %all_gather.3.own), channel_id=1, source_target_pairs={{0,8},{8,0},{1,9},{9,1},{2,10},{10,2},{3,11},{11,3},{4,12},{12,4},... | collective-permute-start | bytes 2359304 | tf_op jit(solution)/shard_map/ppermute | solution.py:234
  45.6 0.0 all-to-all-done.recv
  45.6 0.0 copy-done
  45.6 0.0 copy-done.1
  45.7 2.2 %attend_own.1 = (f32[512,384]{1,0:T(8,128)S(1)}, f32[512,384]{1,0:T(8,128)S(1)}, f32[512,384]{1,0:T(8,128)S(1)}, f32[16,384]{1,0:T(8,128)S(1)}) custom-call(s32[2]{0:T(128)S(1)} %copy-done.1, bf16[32,24,384]{2,1,0:T(8,128)(2,1)S(1)} %all-to-all-done.recv, bf16[512,768]{1,0:T(8,128)(2,1)S(1)} %all_gather.3.own, f32[50,384]{1,0:T(8,128)S(1)} %copy-done), custom_call_target="tpu_custom_call" | custom-call | flops 402653184 | bytes 2097152 | tf_op jit(solution)/shard_map/attend_own/pallas_call | solution.py:237
  47.8 0.0 collective-permute-done.1.other
  47.8 1.6 %attend_other.1 = bf16[32,56,128]{2,1,0:T(8,128)(2,1)S(1)} custom-call(bf16[32,24,384]{2,1,0:T(8,128)(2,1)S(1)} %all-to-all-done.recv, bf16[512,768]{1,0:T(8,128)(2,1)S(1)} %collective-permute-done.1.other, f32[512,384]{1,0:T(8,128)S(1)} %get-tuple-element.10.acc_in, f32[512,384]{1,0:T(8,128)S(1)} %get-tuple-element.11.top_in, ...), custom_call_target="tpu_custom_call" | custom-call | flops 402653184 | bytes 2097152 | tf_op jit(solution)/shard_map/attend_other/pallas_call | solution.py:246
  49.5 25.2 %all_to_all.10.recv = bf16[32,56,128]{2,1,0:T(8,128)(2,1)S(1)} all-to-all(bf16[32,56,128]{2,1,0:T(8,128)(2,1)S(1)} %attend_other.1), channel_id=1, replica_groups=mesh['zq'=4,'zp'=2,'y'=4,'c'=2,'h'=2,'x'=4] {'y','h','x'}, dimensions={0} | all-to-all | bytes 917504 | tf_op jit(solution)/shard_map/all_to_all | solution.py:255
  74.7 1.1 %merge.1 = (bf16[8,3072]{1,0:T(8,128)(2,1)}, bf16[8,3072]{1,0:T(8,128)(2,1)}) custom-call(bf16[32,56,128]{2,1,0:T(8,128)(2,1)S(1)} %all_to_all.10.recv), custom_call_target="tpu_custom_call" | custom-call | tf_op jit(solution)/shard_map/merge/pallas_call | solution.py:256
  (1 shorter events, 0.0 us)
Async XLA Ops:
  2.6 14.7 %collective-permute-start = (bf16[64,768]{1,0:T(8,128)(2,1)}, bf16[64,768]{1,0:T(8,128)(2,1)S(1)}, u32[]{:S(2)}, u32[]{:S(2)}) collective-permute-start(bf16[64,768]{1,0:T(8,128)(2,1)} %get-tuple-element.9), channel_id=1, source_target_pairs={{0,64},{64,0},{1,65},{65,1},{2,66},{66,2},{3,67},{67,3},{4,68},{68... | collective-permute-start | bytes 294920 | tf_op jit(solution)/shard_map/ppermute | solution.py:232
  7.4 9.8 %copy-start.2 = (bf16[64,768]{1,0:T(8,128)(2,1)S(1)}, bf16[64,768]{1,0:T(8,128)(2,1)}, u32[]{:S(2)}) copy-start(bf16[64,768]{1,0:T(8,128)(2,1)} %get-tuple-element.9) | copy-start | bytes 294916
  7.5 38.2 %all-to-all-start = ((bf16[32,24,384]{2,1,0:T(8,128)(2,1)}), bf16[32,24,384]{2,1,0:T(8,128)(2,1)S(1)}, u32[]{:S(2)}, u32[]{:S(2)}) async-start(bf16[32,24,384]{2,1,0:T(8,128)(2,1)} %get-tuple-element.8), calls=%async_computation | async-start | bytes 1179648 | tf_op jit(solution)/shard_map/all_to_all | solution.py:231
  17.3 28.3 %copy-start = (f32[50,384]{1,0:T(8,128)S(1)}, f32[50,384]{1,0:T(8,128)}, u32[]{:S(2)}) copy-start(f32[50,384]{1,0:T(8,128)} %gates.1) | copy-start | bytes 230404
  17.3 28.3 %copy-start.1 = (s32[2]{0:T(128)S(1)}, s32[2]{0:T(128)}, u32[]{:S(2)}) copy-start(s32[2]{0:T(128)} %step_ref.1) | copy-start | bytes 28
  40.5 7.3 %collective-permute-start.1 = (bf16[512,768]{1,0:T(8,128)(2,1)S(1)}, bf16[512,768]{1,0:T(8,128)(2,1)S(1)}, u32[]{:S(2)}, u32[]{:S(2)}) collective-permute-start(bf16[512,768]{1,0:T(8,128)(2,1)S(1)} %all_gather.3.own), channel_id=1, source_target_pairs={{0,8},{8,0},{1,9},{9,1},{2,10},{10,2},{3,11},{11,3},{4,12},{12,4},... | collective-permute-start | bytes 2359304 | tf_op jit(solution)/shard_map/ppermute | solution.py:234

commit v5 on v4

--- a/solution.py
+++ b/solution.py
@@ -18,7 +18,7 @@
 PATCH = TOK * NHEAD
 FRESH = 2 * TOK // NY
 BLOCK = 2 * TOK + 2 * FRESH
-SENT = 2 * TOK * GROUP + TOK
+SENT = TOK * GROUP + 1
 SCALE2 = HDIM ** (-0.5) * 1.4426950408889634
 LN2 = 0.6931471805599453
 NEG = -1e30
@@ -135,10 +135,15 @@
         acc_out[:, head_cols(head)] = acc + jnp.concatenate(accs, axis=0)
 
 
+def fold_matrix(height, width, short, long):
+    at = lax.broadcasted_iota(jnp.int32, (height, width), short)
+    row = lax.broadcasted_iota(jnp.int32, (height, width), long)
+    return jnp.where(at == 2 * (row // (2 * TOK)) + row % 2, 1.0, 0.0).astype(BF16)
+
+
 def attend_other_kernel(recv, other, acc_in, top_in, total_in, gate_in, out):
     lane = lax.broadcasted_iota(jnp.int32, (ROWS, HDIM), 1)
-    step_of_row = (lax.broadcasted_iota(jnp.int32, (ROWS, HDIM), 0) // TOK) % 2
-    slot = lane - 3 * GROUP * step_of_row
+    slot = lane - 3 * GROUP * (lax.broadcasted_iota(jnp.int32, (ROWS, HDIM), 0) // 2 % TOK)
     stats = [jnp.zeros((ROWS, HDIM), F32) for _ in range(NY)]
 
     def scores(head):
@@ -166,43 +171,50 @@
         for y in range(NY):
             total = acc[patch_rows(y)] + keeps[y] * acc_in[patch_rows(y), cols]
             mixed = (total / totals[y]) * gate
-            out[y * NHEAD : (y + 1) * NHEAD, head * 2 * TOK : (head + 1) * 2 * TOK, :] = (
-                mixed.astype(BF16).reshape(NHEAD, 2 * TOK, HDIM)
-            )
+            mixed = mixed.astype(BF16)
+            for i in range(NHEAD):
+                start = 2 * SENT * (i * NY + y) + 2 * TOK * head
+                out[start : start + 2 * TOK, :] = mixed[2 * TOK * i : 2 * TOK * (i + 1)]
             size = tops[y] * SCALE2 + jnp.log(totals[y]) * (1.0 / LN2)
             for i, piece in enumerate(split3(size)):
                 stats[y] = jnp.where(slot == 3 * head + i, piece.astype(F32), stats[y])
     for y in range(NY):
-        folded = jnp.sum(stats[y].reshape(NHEAD, 2, TOK, HDIM), axis=1)
-        out[y * NHEAD : (y + 1) * NHEAD, SENT - TOK : SENT, :] = folded.astype(BF16)
+        for i in range(NHEAD):
+            rows = stats[y][2 * TOK * i : 2 * TOK * i + TOK] + stats[y][2 * TOK * i + TOK : 2 * TOK * (i + 1)]
+            rows = rows + pltpu.roll(rows, 4, 0)
+            rows = rows + pltpu.roll(rows, 2, 0)
+            start = 2 * SENT * (i * NY + y) + 2 * TOK * GROUP
+            out[start : start + 2, :] = rows[0:2].astype(BF16)
 
 
 def merge_kernel(recv, out_first, out_second):
-    at = lax.broadcasted_iota(jnp.int32, (HDIM, 2 * WIDTH), 0)
-    to = lax.broadcasted_iota(jnp.int32, (HDIM, 2 * WIDTH), 1)
-    spread = jnp.where(at // 3 == to // HDIM, 1.0, 0.0).astype(BF16)
-    sizes, parts = [], []
-    for y in range(NY):
-        blocks = slice(y * NHEAD, (y + 1) * NHEAD)
-        stats = recv[blocks, SENT - TOK : SENT, :].astype(F32).reshape(NHEAD * TOK, HDIM).astype(BF16)
-        sizes.append(jnp.dot(stats, spread, preferred_element_type=F32))
-        parts.append(recv[blocks, 0 : SENT - TOK, :].astype(F32))
-    for step, out in ((0, out_first), (1, out_second)):
-        for head in range(GROUP):
-            lanes = slice((step * GROUP + head) * HDIM, (step * GROUP + head + 1) * HDIM)
-            rows = slice((2 * head + step) * TOK, (2 * head + step + 1) * TOK)
-            size = [s[:, lanes] for s in sizes]
-            top = functools.reduce(jnp.maximum, size)
-            total = jnp.zeros_like(top)
-            acc = jnp.zeros_like(top)
-            for y in range(NY):
-                weight = jnp.exp2(size[y] - top)
-                total = total + weight
-                acc = acc + weight * parts[y][:, rows, :].reshape(NHEAD * TOK, HDIM)
-            result = (acc / total).astype(BF16)
-            for g in range(NHEAD):
-                cols = slice(g * WIDTH + head * HDIM, g * WIDTH + (head + 1) * HDIM)
-                out[:, cols] = result[g * TOK : (g + 1) * TOK]
+    at = lax.broadcasted_iota(jnp.int32, (HDIM, WIDTH), 0)
+    to = lax.broadcasted_iota(jnp.int32, (HDIM, WIDTH), 1)
+    spread = jnp.where((at % (3 * GROUP)) // 3 == to // HDIM, 1.0, 0.0).astype(BF16)
+    lane = lax.broadcasted_iota(jnp.int32, (ALL, HDIM), 1)
+    pair = lax.broadcasted_iota(jnp.int32, (ALL, HDIM), 0) // 2 % TOK
+    stats = jnp.concatenate(
+        [recv[pl.ds(2 * SENT * (i * NY + y + 1) - 2, 2), :] for y in range(NY) for i in range(NHEAD)], axis=0
+    )
+    stats = jnp.dot(fold_matrix(ALL, 2 * PEERS, 1, 0), stats, preferred_element_type=F32)
+    stats = jnp.where(lane // (3 * GROUP) == pair, stats, 0.0).astype(BF16)
+    sizes = jnp.dot(stats, spread, preferred_element_type=F32)
+    for head in range(GROUP):
+        size = [sizes[patch_rows(y), head_cols(head)] for y in range(NY)]
+        top = functools.reduce(jnp.maximum, size)
+        total = jnp.zeros_like(top)
+        acc = jnp.zeros_like(top)
+        for y in range(NY):
+            weight = jnp.exp2(size[y] - top)
+            total = total + weight
+            starts = [2 * SENT * (i * NY + y) + 2 * TOK * head for i in range(NHEAD)]
+            part = jnp.concatenate([recv[a : a + 2 * TOK, :] for a in starts], axis=0)
+            acc = acc + weight * part.astype(F32)
+        result = acc / total
+        for g in range(NHEAD):
+            cols = slice(g * WIDTH + head * HDIM, g * WIDTH + (head + 1) * HDIM)
+            out_first[:, cols] = result[g * 2 * TOK : g * 2 * TOK + TOK].astype(BF16)
+            out_second[:, cols] = result[g * 2 * TOK + TOK : (g + 1) * 2 * TOK].astype(BF16)
 
 
 def vmem(n):
@@ -245,14 +257,16 @@
     )(step_index, recv, own, gate_table)
     partial = pl.pallas_call(
         attend_other_kernel,
-        out_shape=shape((PEERS, SENT, HDIM), BF16),
+        out_shape=shape((2 * SENT * PEERS, HDIM), BF16),
         in_specs=vmem(6),
         out_specs=vmem(1)[0],
         compiler_params=PARAMS,
         cost_estimate=cost,
         name="attend_other",
     )(recv, other, *state)
-    back = lax.all_to_all(partial, PLANE, split_axis=0, concat_axis=0, tiled=True)
+    back = lax.all_to_all(
+        partial.reshape((PEERS, SENT, 2, HDIM)), ("h", "x", "y"), split_axis=0, concat_axis=0, tiled=True
+    ).reshape(partial.shape)
     return pl.pallas_call(
         merge_kernel,
         out_shape=(shape((TOK, NHEAD * WIDTH), BF16),) * 2,

time: 76.1 us -> 75.6 us (level)
  blocking collectives: 48.4 us -> 47.6 us
where the time goes in v5:
time: 75.6 us; the launch traced here: 75.2 us
  blocking collectives  47.6 us (63%)
  starting transfers between devices  19.8 us (26%)
  Pallas kernels  7.03 us (9%)
  between operations  0.76 us (1%)
    all_to_all x1, blocking collectives, body(): lax.all_to_all(partial.reshape((PEERS, SENT, 2, HDIM)), ('h', 'x', 'y'),...  24.5 us
    all_gather x1, blocking collectives, body(): lax.all_gather(jnp.concatenate([kv, pair], axis=0), 'zq', axis=0, tiled=T...  23.2 us
    all_to_all x1, starting transfers between devices, body(): lax.all_to_all(packed, PLANE, split_axis=0, concat_axis=0, tiled=True)  9.81 us
    ppermute x1, starting transfers between devices, body(): other = lax.ppermute(own, 'c', [(0, 1), (1, 0)])  5.13 us
    ppermute x1, starting transfers between devices, body(): pair = lax.ppermute(kv, 'zp', [(0, 1), (1, 0)])  4.83 us
    pallas_call x1, Pallas kernels, body(): pl.pallas_call(attend_own_kernel, out_shape=state, in_specs=smem(1) + vme...  2.16 us
    pallas_call x1, Pallas kernels, body(): pl.pallas_call(pack_kernel, out_shape=(shape((PEERS, BLOCK, WIDTH), BF16)...  1.96 us
    pallas_call x1, Pallas kernels, body(): pl.pallas_call(attend_other_kernel, out_shape=shape((2 * SENT * PEERS, HD...  1.72 us
  transfers between devices with their start and end apart: 3, of which 0 were waited for; matrix products, arithmetic and copies ran while one was open for 0% of the time, Pallas kernels for 3%

profile of v5, /device:TPU:1, one launch (start us, length us, event | category | flops | bytes accessed | tf_op | source)
XLA Modules:
  0.0 75.2 jit_solution(1092029570714598368)
XLA Ops:
  0.6 2.0 %pack.1 = (bf16[32,24,384]{2,1,0:T(8,128)(2,1)}, bf16[64,768]{1,0:T(8,128)(2,1)}) custom-call(bf16[8,3072]{1,0:T(8,128)(2,1)} %q1.1, bf16[8,3072]{1,0:T(8,128)(2,1)} %k1.1, bf16[8,3072]{1,0:T(8,128)(2,1)} %v1.1, bf16[8,3072]{1,0:T(8,128)(2,1)} %q2.1, bf16[8,3072]{1,0:T(8,128)(2,1)} %k2.1, bf16[8,3072]{1,0:T(8,128)(2,1)} %v2.1, bf16[64,384]{1,0:T(8,128)(2,1)} %ks.1, ...), custom_call_target="tpu_custom_call" | custom-call | tf_op jit(solution)/shard_map/pack/pallas_call | solution.py:234
  2.6 4.8 %collective-permute-start = (bf16[64,768]{1,0:T(8,128)(2,1)}, bf16[64,768]{1,0:T(8,128)(2,1)S(1)}, u32[]{:S(2)}, u32[]{:S(2)}) collective-permute-start(bf16[64,768]{1,0:T(8,128)(2,1)} %get-tuple-element.9), channel_id=1, source_target_pairs={{0,64},{64,0},{1,65},{65,1},{2,66},{66,2},{3,67},{67,3},{4,68},{68... | collective-permute-start | bytes 294920 | tf_op jit(solution)/shard_map/ppermute | solution.py:244
  7.4 0.0 copy-start.2
  7.5 9.8 %all-to-all-start = ((bf16[32,24,384]{2,1,0:T(8,128)(2,1)}), bf16[32,24,384]{2,1,0:T(8,128)(2,1)S(1)}, u32[]{:S(2)}, u32[]{:S(2)}) async-start(bf16[32,24,384]{2,1,0:T(8,128)(2,1)} %get-tuple-element.8), calls=%async_computation | async-start | bytes 1179648 | tf_op jit(solution)/shard_map/all_to_all | solution.py:243
  17.3 0.0 collective-permute-done
  17.3 0.0 copy-done.2
  17.3 0.0 copy-start
  17.3 0.0 copy-start.1
  17.3 23.2 %all_gather.3.own = bf16[512,768]{1,0:T(8,128)(2,1)S(1)} all-gather(bf16[128,768]{1,0:T(8,128)(2,1)S(1)} %pad_maximum_fusion), channel_id=1, replica_groups=mesh['zq'=4,'zp'=2,'y'=4,'c'=2,'h'=2,'x'=4] {'zq'}, dimensions={0}, use_global_device_ids=true | all-gather | bytes 983040 | tf_op jit(solution)/shard_map/all_gather | solution.py:245
  40.5 5.1 %collective-permute-start.1 = (bf16[512,768]{1,0:T(8,128)(2,1)S(1)}, bf16[512,768]{1,0:T(8,128)(2,1)S(1)}, u32[]{:S(2)}, u32[]{:S(2)}) collective-permute-start(bf16[512,768]{1,0:T(8,128)(2,1)S(1)} %all_gather.3.own), channel_id=1, source_target_pairs={{0,8},{8,0},{1,9},{9,1},{2,10},{10,2},{3,11},{11,3},{4,12},{12,4},... | collective-permute-start | bytes 2359304 | tf_op jit(solution)/shard_map/ppermute | solution.py:246
  45.6 0.0 all-to-all-done.recv
  45.6 0.0 copy-done
  45.6 0.0 copy-done.1
  45.7 2.2 %attend_own.1 = (f32[512,384]{1,0:T(8,128)S(1)}, f32[512,384]{1,0:T(8,128)S(1)}, f32[512,384]{1,0:T(8,128)S(1)}, f32[16,384]{1,0:T(8,128)S(1)}) custom-call(s32[2]{0:T(128)S(1)} %copy-done.1, bf16[32,24,384]{2,1,0:T(8,128)(2,1)S(1)} %all-to-all-done.recv, bf16[512,768]{1,0:T(8,128)(2,1)S(1)} %all_gather.3.own, f32[50,384]{1,0:T(8,128)S(1)} %copy-done), custom_call_target="tpu_custom_call" | custom-call | flops 402653184 | bytes 2097152 | tf_op jit(solution)/shard_map/attend_own/pallas_call | solution.py:249
  47.8 0.0 collective-permute-done.1.other
  47.8 1.7 %attend_other.1 = bf16[1600,128]{1,0:T(8,128)(2,1)S(1)} custom-call(bf16[32,24,384]{2,1,0:T(8,128)(2,1)S(1)} %all-to-all-done.recv, bf16[512,768]{1,0:T(8,128)(2,1)S(1)} %collective-permute-done.1.other, f32[512,384]{1,0:T(8,128)S(1)} %get-tuple-element.10.acc_in, f32[512,384]{1,0:T(8,128)S(1)} %get-tuple-element.11.top_in, ...), custom_call_target="tpu_custom_call" | custom-call | flops 402653184 | bytes 2097152 | tf_op jit(solution)/shard_map/attend_other/pallas_call | solution.py:258
  49.6 24.5 %all_to_all.10 = bf16[32,25,2,128]{3,2,1,0:T(2,128)(2,1)S(1)} all-to-all(bf16[32,25,2,128]{3,2,1,0:T(2,128)(2,1)S(1)} %bitcast.3), channel_id=1, replica_groups=mesh['zq'=4,'zp'=2,'y'=4,'c'=2,'h'=2,'x'=4] {'h','x','y'}, dimensions={0} | all-to-all | bytes 819200 | tf_op jit(solution)/shard_map/all_to_all | solution.py:267
  74.1 1.2 %merge.1 = (bf16[8,3072]{1,0:T(8,128)(2,1)}, bf16[8,3072]{1,0:T(8,128)(2,1)}) custom-call(bf16[1600,128]{1,0:T(8,128)(2,1)S(1)} %bitcast.2), custom_call_target="tpu_custom_call" | custom-call | tf_op jit(solution)/shard_map/merge/pallas_call | solution.py:270
  (1 shorter events, 0.0 us)
Async XLA Ops:
  2.6 14.7 %collective-permute-start = (bf16[64,768]{1,0:T(8,128)(2,1)}, bf16[64,768]{1,0:T(8,128)(2,1)S(1)}, u32[]{:S(2)}, u32[]{:S(2)}) collective-permute-start(bf16[64,768]{1,0:T(8,128)(2,1)} %get-tuple-element.9), channel_id=1, source_target_pairs={{0,64},{64,0},{1,65},{65,1},{2,66},{66,2},{3,67},{67,3},{4,68},{68... | collective-permute-start | bytes 294920 | tf_op jit(solution)/shard_map/ppermute | solution.py:244
  7.4 9.8 %copy-start.2 = (bf16[64,768]{1,0:T(8,128)(2,1)S(1)}, bf16[64,768]{1,0:T(8,128)(2,1)}, u32[]{:S(2)}) copy-start(bf16[64,768]{1,0:T(8,128)(2,1)} %get-tuple-element.9) | copy-start | bytes 294916
  7.5 38.2 %all-to-all-start = ((bf16[32,24,384]{2,1,0:T(8,128)(2,1)}), bf16[32,24,384]{2,1,0:T(8,128)(2,1)S(1)}, u32[]{:S(2)}, u32[]{:S(2)}) async-start(bf16[32,24,384]{2,1,0:T(8,128)(2,1)} %get-tuple-element.8), calls=%async_computation | async-start | bytes 1179648 | tf_op jit(solution)/shard_map/all_to_all | solution.py:243
  17.3 28.3 %copy-start = (f32[50,384]{1,0:T(8,128)S(1)}, f32[50,384]{1,0:T(8,128)}, u32[]{:S(2)}) copy-start(f32[50,384]{1,0:T(8,128)} %gates.1) | copy-start | bytes 230404
  17.3 28.3 %copy-start.1 = (s32[2]{0:T(128)S(1)}, s32[2]{0:T(128)}, u32[]{:S(2)}) copy-start(s32[2]{0:T(128)} %step_ref.1) | copy-start | bytes 28
  40.5 7.3 %collective-permute-start.1 = (bf16[512,768]{1,0:T(8,128)(2,1)S(1)}, bf16[512,768]{1,0:T(8,128)(2,1)S(1)}, u32[]{:S(2)}, u32[]{:S(2)}) collective-permute-start(bf16[512,768]{1,0:T(8,128)(2,1)S(1)} %all_gather.3.own), channel_id=1, source_target_pairs={{0,8},{8,0},{1,9},{9,1},{2,10},{10,2},{3,11},{11,3},{4,12},{12,4},... | collective-permute-start | bytes 2359304 | tf_op jit(solution)/shard_map/ppermute | solution.py:246

commit v6 on v5

--- a/solution.py
+++ b/solution.py
@@ -171,10 +171,9 @@
         for y in range(NY):
             total = acc[patch_rows(y)] + keeps[y] * acc_in[patch_rows(y), cols]
             mixed = (total / totals[y]) * gate
-            mixed = mixed.astype(BF16)
-            for i in range(NHEAD):
-                start = 2 * SENT * (i * NY + y) + 2 * TOK * head
-                out[start : start + 2 * TOK, :] = mixed[2 * TOK * i : 2 * TOK * (i + 1)]
+            out[:, y, head * TOK : (head + 1) * TOK, :, :] = (
+                mixed.astype(BF16).reshape(NHEAD, TOK, 2, HDIM)
+            )
             size = tops[y] * SCALE2 + jnp.log(totals[y]) * (1.0 / LN2)
             for i, piece in enumerate(split3(size)):
                 stats[y] = jnp.where(slot == 3 * head + i, piece.astype(F32), stats[y])
@@ -183,8 +182,7 @@
             rows = stats[y][2 * TOK * i : 2 * TOK * i + TOK] + stats[y][2 * TOK * i + TOK : 2 * TOK * (i + 1)]
             rows = rows + pltpu.roll(rows, 4, 0)
             rows = rows + pltpu.roll(rows, 2, 0)
-            start = 2 * SENT * (i * NY + y) + 2 * TOK * GROUP
-            out[start : start + 2, :] = rows[0:2].astype(BF16)
+            out[i, y, SENT - 1, :, :] = rows[0:2].astype(BF16)
 
 
 def merge_kernel(recv, out_first, out_second):
@@ -193,9 +191,7 @@
     spread = jnp.where((at % (3 * GROUP)) // 3 == to // HDIM, 1.0, 0.0).astype(BF16)
     lane = lax.broadcasted_iota(jnp.int32, (ALL, HDIM), 1)
     pair = lax.broadcasted_iota(jnp.int32, (ALL, HDIM), 0) // 2 % TOK
-    stats = jnp.concatenate(
-        [recv[pl.ds(2 * SENT * (i * NY + y + 1) - 2, 2), :] for y in range(NY) for i in range(NHEAD)], axis=0
-    )
+    stats = jnp.concatenate([recv[:, y, SENT - 1, :, :].reshape(2 * NHEAD, HDIM) for y in range(NY)], axis=0)
     stats = jnp.dot(fold_matrix(ALL, 2 * PEERS, 1, 0), stats, preferred_element_type=F32)
     stats = jnp.where(lane // (3 * GROUP) == pair, stats, 0.0).astype(BF16)
     sizes = jnp.dot(stats, spread, preferred_element_type=F32)
@@ -207,8 +203,7 @@
         for y in range(NY):
             weight = jnp.exp2(size[y] - top)
             total = total + weight
-            starts = [2 * SENT * (i * NY + y) + 2 * TOK * head for i in range(NHEAD)]
-            part = jnp.concatenate([recv[a : a + 2 * TOK, :] for a in starts], axis=0)
+            part = recv[:, y, head * TOK : (head + 1) * TOK, :, :].reshape(ROWS, HDIM)
             acc = acc + weight * part.astype(F32)
         result = acc / total
         for g in range(NHEAD):
@@ -257,7 +252,7 @@
     )(step_index, recv, own, gate_table)
     partial = pl.pallas_call(
         attend_other_kernel,
-        out_shape=shape((2 * SENT * PEERS, HDIM), BF16),
+        out_shape=shape((NHEAD, NY, SENT, 2, HDIM), BF16),
         in_specs=vmem(6),
         out_specs=vmem(1)[0],
         compiler_params=PARAMS,
@@ -265,7 +260,7 @@
         name="attend_other",
     )(recv, other, *state)
     back = lax.all_to_all(
-        partial.reshape((PEERS, SENT, 2, HDIM)), ("h", "x", "y"), split_axis=0, concat_axis=0, tiled=True
+        partial.reshape((PEERS,) + partial.shape[2:]), ("h", "x", "y"), split_axis=0, concat_axis=0, tiled=True
     ).reshape(partial.shape)
     return pl.pallas_call(
         merge_kernel,

time: 75.6 us -> 75.9 us (level)
  no operation moved by 1% of the time
where the time goes in v6:
time: 75.9 us; the launch traced here: 75.5 us
  blocking collectives  47.6 us (63%)
  starting transfers between devices  19.8 us (26%)
  Pallas kernels  7.28 us (10%)
  between operations  0.76 us (1%)
    all_to_all x1, blocking collectives, body(): lax.all_to_all(partial.reshape((PEERS,) + partial.shape[2:]), ('h', 'x',...  24.5 us
    all_gather x1, blocking collectives, body(): lax.all_gather(jnp.concatenate([kv, pair], axis=0), 'zq', axis=0, tiled=T...  23.2 us
    all_to_all x1, starting transfers between devices, body(): lax.all_to_all(packed, PLANE, split_axis=0, concat_axis=0, tiled=True)  9.81 us
    ppermute x1, starting transfers between devices, body(): other = lax.ppermute(own, 'c', [(0, 1), (1, 0)])  5.13 us
    ppermute x1, starting transfers between devices, body(): pair = lax.ppermute(kv, 'zp', [(0, 1), (1, 0)])  4.83 us
    pallas_call x1, Pallas kernels, body(): pl.pallas_call(attend_own_kernel, out_shape=state, in_specs=smem(1) + vme...  2.16 us
    pallas_call x1, Pallas kernels, body(): pl.pallas_call(pack_kernel, out_shape=(shape((PEERS, BLOCK, WIDTH), BF16)...  1.96 us
    pallas_call x1, Pallas kernels, body(): pl.pallas_call(attend_other_kernel, out_shape=shape((NHEAD, NY, SENT, 2,...  1.85 us
  transfers between devices with their start and end apart: 3, of which 0 were waited for; matrix products, arithmetic and copies ran while one was open for 0% of the time, Pallas kernels for 3%

profile of v6, /device:TPU:1, one launch (start us, length us, event | category | flops | bytes accessed | tf_op | source)
XLA Modules:
  0.0 75.5 jit_solution(1303611580956810661)
XLA Ops:
  0.6 2.0 %pack.1 = (bf16[32,24,384]{2,1,0:T(8,128)(2,1)}, bf16[64,768]{1,0:T(8,128)(2,1)}) custom-call(bf16[8,3072]{1,0:T(8,128)(2,1)} %q1.1, bf16[8,3072]{1,0:T(8,128)(2,1)} %k1.1, bf16[8,3072]{1,0:T(8,128)(2,1)} %v1.1, bf16[8,3072]{1,0:T(8,128)(2,1)} %q2.1, bf16[8,3072]{1,0:T(8,128)(2,1)} %k2.1, bf16[8,3072]{1,0:T(8,128)(2,1)} %v2.1, bf16[64,384]{1,0:T(8,128)(2,1)} %ks.1, ...), custom_call_target="tpu_custom_call" | custom-call | tf_op jit(solution)/shard_map/pack/pallas_call | solution.py:229
  2.6 4.8 %collective-permute-start = (bf16[64,768]{1,0:T(8,128)(2,1)}, bf16[64,768]{1,0:T(8,128)(2,1)S(1)}, u32[]{:S(2)}, u32[]{:S(2)}) collective-permute-start(bf16[64,768]{1,0:T(8,128)(2,1)} %get-tuple-element.9), channel_id=1, source_target_pairs={{0,64},{64,0},{1,65},{65,1},{2,66},{66,2},{3,67},{67,3},{4,68},{68... | collective-permute-start | bytes 294920 | tf_op jit(solution)/shard_map/ppermute | solution.py:239
  7.4 0.0 copy-start.2
  7.5 9.8 %all-to-all-start = ((bf16[32,24,384]{2,1,0:T(8,128)(2,1)}), bf16[32,24,384]{2,1,0:T(8,128)(2,1)S(1)}, u32[]{:S(2)}, u32[]{:S(2)}) async-start(bf16[32,24,384]{2,1,0:T(8,128)(2,1)} %get-tuple-element.8), calls=%async_computation | async-start | bytes 1179648 | tf_op jit(solution)/shard_map/all_to_all | solution.py:238
  17.3 0.0 collective-permute-done
  17.3 0.0 copy-done.2
  17.3 0.0 copy-start
  17.3 0.0 copy-start.1
  17.3 23.2 %all_gather.3.own = bf16[512,768]{1,0:T(8,128)(2,1)S(1)} all-gather(bf16[128,768]{1,0:T(8,128)(2,1)S(1)} %pad_maximum_fusion), channel_id=1, replica_groups=mesh['zq'=4,'zp'=2,'y'=4,'c'=2,'h'=2,'x'=4] {'zq'}, dimensions={0}, use_global_device_ids=true | all-gather | bytes 983040 | tf_op jit(solution)/shard_map/all_gather | solution.py:240
  40.5 5.1 %collective-permute-start.1 = (bf16[512,768]{1,0:T(8,128)(2,1)S(1)}, bf16[512,768]{1,0:T(8,128)(2,1)S(1)}, u32[]{:S(2)}, u32[]{:S(2)}) collective-permute-start(bf16[512,768]{1,0:T(8,128)(2,1)S(1)} %all_gather.3.own), channel_id=1, source_target_pairs={{0,8},{8,0},{1,9},{9,1},{2,10},{10,2},{3,11},{11,3},{4,12},{12,4},... | collective-permute-start | bytes 2359304 | tf_op jit(solution)/shard_map/ppermute | solution.py:241
  45.6 0.0 all-to-all-done.recv
  45.6 0.0 copy-done
  45.6 0.0 copy-done.1
  45.7 2.2 %attend_own.1 = (f32[512,384]{1,0:T(8,128)S(1)}, f32[512,384]{1,0:T(8,128)S(1)}, f32[512,384]{1,0:T(8,128)S(1)}, f32[16,384]{1,0:T(8,128)S(1)}) custom-call(s32[2]{0:T(128)S(1)} %copy-done.1, bf16[32,24,384]{2,1,0:T(8,128)(2,1)S(1)} %all-to-all-done.recv, bf16[512,768]{1,0:T(8,128)(2,1)S(1)} %all_gather.3.own, f32[50,384]{1,0:T(8,128)S(1)} %copy-done), custom_call_target="tpu_custom_call" | custom-call | flops 402653184 | bytes 2097152 | tf_op jit(solution)/shard_map/attend_own/pallas_call | solution.py:244
  47.8 0.0 collective-permute-done.1.other
  47.8 1.8 %attend_other.1 = bf16[8,4,25,2,128]{4,3,2,1,0:T(2,128)(2,1)S(1)} custom-call(bf16[32,24,384]{2,1,0:T(8,128)(2,1)S(1)} %all-to-all-done.recv, bf16[512,768]{1,0:T(8,128)(2,1)S(1)} %collective-permute-done.1.other, f32[512,384]{1,0:T(8,128)S(1)} %get-tuple-element.10.acc_in, f32[512,384]{1,0:T(8,128)S(1)} %get-tuple-element.11.top_in, ...), custom_call_target="tpu_custom_call" | custom-call | flops 402653184 | bytes 2097152 | tf_op jit(solution)/shard_map/attend_other/pallas_call | solution.py:253
  49.7 24.5 %all_to_all.10 = bf16[32,25,2,128]{3,2,1,0:T(2,128)(2,1)S(1)} all-to-all(bf16[32,25,2,128]{3,2,1,0:T(2,128)(2,1)S(1)} %bitcast.3), channel_id=1, replica_groups=mesh['zq'=4,'zp'=2,'y'=4,'c'=2,'h'=2,'x'=4] {'h','x','y'}, dimensions={0} | all-to-all | bytes 819200 | tf_op jit(solution)/shard_map/all_to_all | solution.py:262
  74.2 1.3 %merge.1 = (bf16[8,3072]{1,0:T(8,128)(2,1)}, bf16[8,3072]{1,0:T(8,128)(2,1)}) custom-call(bf16[8,4,25,2,128]{4,3,2,1,0:T(2,128)(2,1)S(1)} %bitcast.2), custom_call_target="tpu_custom_call" | custom-call | tf_op jit(solution)/shard_map/merge/pallas_call | solution.py:265
  (1 shorter events, 0.0 us)
Async XLA Ops:
  2.6 14.7 %collective-permute-start = (bf16[64,768]{1,0:T(8,128)(2,1)}, bf16[64,768]{1,0:T(8,128)(2,1)S(1)}, u32[]{:S(2)}, u32[]{:S(2)}) collective-permute-start(bf16[64,768]{1,0:T(8,128)(2,1)} %get-tuple-element.9), channel_id=1, source_target_pairs={{0,64},{64,0},{1,65},{65,1},{2,66},{66,2},{3,67},{67,3},{4,68},{68... | collective-permute-start | bytes 294920 | tf_op jit(solution)/shard_map/ppermute | solution.py:239
  7.4 9.8 %copy-start.2 = (bf16[64,768]{1,0:T(8,128)(2,1)S(1)}, bf16[64,768]{1,0:T(8,128)(2,1)}, u32[]{:S(2)}) copy-start(bf16[64,768]{1,0:T(8,128)(2,1)} %get-tuple-element.9) | copy-start | bytes 294916
  7.5 38.2 %all-to-all-start = ((bf16[32,24,384]{2,1,0:T(8,128)(2,1)}), bf16[32,24,384]{2,1,0:T(8,128)(2,1)S(1)}, u32[]{:S(2)}, u32[]{:S(2)}) async-start(bf16[32,24,384]{2,1,0:T(8,128)(2,1)} %get-tuple-element.8), calls=%async_computation | async-start | bytes 1179648 | tf_op jit(solution)/shard_map/all_to_all | solution.py:238
  17.3 28.3 %copy-start = (f32[50,384]{1,0:T(8,128)S(1)}, f32[50,384]{1,0:T(8,128)}, u32[]{:S(2)}) copy-start(f32[50,384]{1,0:T(8,128)} %gates.1) | copy-start | bytes 230404
  17.3 28.3 %copy-start.1 = (s32[2]{0:T(128)S(1)}, s32[2]{0:T(128)}, u32[]{:S(2)}) copy-start(s32[2]{0:T(128)} %step_ref.1) | copy-start | bytes 28
  40.5 7.3 %collective-permute-start.1 = (bf16[512,768]{1,0:T(8,128)(2,1)S(1)}, bf16[512,768]{1,0:T(8,128)(2,1)S(1)}, u32[]{:S(2)}, u32[]{:S(2)}) collective-permute-start(bf16[512,768]{1,0:T(8,128)(2,1)S(1)} %all_gather.3.own), channel_id=1, source_target_pairs={{0,8},{8,0},{1,9},{9,1},{2,10},{10,2},{3,11},{11,3},{4,12},{12,4},... | collective-permute-start | bytes 2359304 | tf_op jit(solution)/shard_map/ppermute | solution.py:241

commit v7 on v6

--- a/solution.py
+++ b/solution.py
@@ -24,7 +24,7 @@
 NEG = -1e30
 F32 = jnp.float32
 BF16 = jnp.bfloat16
-PLANE = ("y", "h", "x")
+PLANE = ("h", "x", "y")
 
 
 def pack_kernel(q1, k1, v1, q2, k2, v2, ks, vs, out, kv, b0, b1, b2, b3, b4, b5, sems):
@@ -43,8 +43,8 @@
         for y in range(NY):
             rows = slice(y * share, (y + 1) * share)
             part = jnp.concatenate([f[rows] for f in fresh], axis=0).astype(BF16)
-            out[y * NHEAD + g, 0 : 2 * TOK, :] = queries
-            out[y * NHEAD + g, 2 * TOK : BLOCK, :] = part
+            out[g, y, 0 : 2 * TOK, :] = queries
+            out[g, y, 2 * TOK : BLOCK, :] = part
 
 
 def split3(x):
@@ -74,7 +74,9 @@
 
 
 def queries_of(recv, head):
-    return recv[:, 0 : 2 * TOK, head_cols(head)].reshape(ALL, HDIM)
+    return jnp.concatenate(
+        [recv[:, y, 0 : 2 * TOK, head_cols(head)].reshape(ROWS, HDIM) for y in range(NY)], axis=0
+    )
 
 
 def patch_rows(y):
@@ -108,7 +110,7 @@
         q = queries_of(recv, head)
         extra = []
         for y in range(NY):
-            fresh = recv[y * NHEAD : (y + 1) * NHEAD, 2 * TOK : BLOCK, head_cols(head)].astype(F32)
+            fresh = recv[:, y, 2 * TOK : BLOCK, head_cols(head)].astype(F32)
             fresh = fresh.reshape(FRESH_ROWS, HDIM).astype(BF16)
             fresh_v = jnp.dot(shift, fresh, preferred_element_type=F32).astype(BF16)
             extra.append((nt_dot(q[patch_rows(y)], fresh) + fresh_bias, fresh_v))
@@ -224,18 +226,23 @@
 PACK_PARAMS = pltpu.CompilerParams(vmem_limit_bytes=62 * 1024 * 1024)
 
 
+def exchange(blocks):
+    flat = blocks.reshape((PEERS,) + blocks.shape[2:])
+    return lax.all_to_all(flat, PLANE, split_axis=0, concat_axis=0, tiled=True).reshape(blocks.shape)
+
+
 def body(q1, k1, v1, q2, k2, v2, key_stale, value_stale, gate_table, step_index):
     shape = jax.ShapeDtypeStruct
     packed, kv = pl.pallas_call(
         pack_kernel,
-        out_shape=(shape((PEERS, BLOCK, WIDTH), BF16), shape((PATCH, 2 * WIDTH), BF16)),
+        out_shape=(shape((NHEAD, NY, BLOCK, WIDTH), BF16), shape((PATCH, 2 * WIDTH), BF16)),
         in_specs=[pl.BlockSpec(memory_space=pltpu.HBM)] * 8,
         out_specs=tuple(vmem(2)),
         scratch_shapes=[pltpu.VMEM((TOK, NHEAD * WIDTH), BF16)] * 6 + [pltpu.SemaphoreType.DMA((8,))],
         compiler_params=PACK_PARAMS,
         name="pack",
     )(q1, k1, v1, q2, k2, v2, key_stale, value_stale)
-    recv = lax.all_to_all(packed, PLANE, split_axis=0, concat_axis=0, tiled=True)
+    recv = exchange(packed)
     pair = lax.ppermute(kv, "zp", [(0, 1), (1, 0)])
     own = lax.all_gather(jnp.concatenate([kv, pair], axis=0), "zq", axis=0, tiled=True)
     other = lax.ppermute(own, "c", [(0, 1), (1, 0)])
@@ -259,9 +266,7 @@
         cost_estimate=cost,
         name="attend_other",
     )(recv, other, *state)
-    back = lax.all_to_all(
-        partial.reshape((PEERS,) + partial.shape[2:]), ("h", "x", "y"), split_axis=0, concat_axis=0, tiled=True
-    ).reshape(partial.shape)
+    back = exchange(partial)
     return pl.pallas_call(
         merge_kernel,
         out_shape=(shape((TOK, NHEAD * WIDTH), BF16),) * 2,

time: 75.9 us -> 75.8 us (level)
  no operation moved by 1% of the time
where the time goes in v7:
time: 75.8 us; the launch traced here: 75.4 us
  blocking collectives  47.7 us (63%)
  starting transfers between devices  19.6 us (26%)
  Pallas kernels  7.3 us (10%)
    all_to_all x1, blocking collectives, exchange(): lax.all_to_all(flat, PLANE, split_axis=0, concat_axis=0, tiled=True)  24.5 us
    all_gather x1, blocking collectives, body(): lax.all_gather(jnp.concatenate([kv, pair], axis=0), 'zq', axis=0, tiled=T...  23.2 us
    all_to_all x1, starting transfers between devices, exchange(): lax.all_to_all(flat, PLANE, split_axis=0, concat_axis=0, tiled=True)  9.81 us
    ppermute x1, starting transfers between devices, body(): other = lax.ppermute(own, 'c', [(0, 1), (1, 0)])  4.99 us
    ppermute x1, starting transfers between devices, body(): pair = lax.ppermute(kv, 'zp', [(0, 1), (1, 0)])  4.83 us
    pallas_call x1, Pallas kernels, body(): pl.pallas_call(attend_own_kernel, out_shape=state, in_specs=smem(1) + vme...  2.17 us
    pallas_call x1, Pallas kernels, body(): pl.pallas_call(pack_kernel, out_shape=(shape((NHEAD, NY, BLOCK, WIDTH), B...  1.96 us
    pallas_call x1, Pallas kernels, body(): pl.pallas_call(attend_other_kernel, out_shape=shape((NHEAD, NY, SENT, 2,...  1.85 us
  transfers between devices with their start and end apart: 3, of which 0 were waited for; matrix products, arithmetic and copies ran while one was open for 0% of the time, Pallas kernels for 3%

profile of v7, /device:TPU:1, one launch (start us, length us, event | category | flops | bytes accessed | tf_op | source)
XLA Modules:
  0.0 75.4 jit_solution(12683279978122599555)
XLA Ops:
  0.6 2.0 %pack.1 = (bf16[8,4,24,384]{3,2,1,0:T(8,128)(2,1)}, bf16[64,768]{1,0:T(8,128)(2,1)}) custom-call(bf16[8,3072]{1,0:T(8,128)(2,1)} %q1.1, bf16[8,3072]{1,0:T(8,128)(2,1)} %k1.1, bf16[8,3072]{1,0:T(8,128)(2,1)} %v1.1, bf16[8,3072]{1,0:T(8,128)(2,1)} %q2.1, bf16[8,3072]{1,0:T(8,128)(2,1)} %k2.1, bf16[8,3072]{1,0:T(8,128)(2,1)} %v2.1, bf16[64,384]{1,0:T(8,128)(2,1)} %ks.1, ...), custom_call_target="tpu_custom_call" | custom-call | tf_op jit(solution)/shard_map/pack/pallas_call | solution.py:236
  2.6 4.8 %collective-permute-start = (bf16[64,768]{1,0:T(8,128)(2,1)}, bf16[64,768]{1,0:T(8,128)(2,1)S(1)}, u32[]{:S(2)}, u32[]{:S(2)}) collective-permute-start(bf16[64,768]{1,0:T(8,128)(2,1)} %get-tuple-element.9), channel_id=1, source_target_pairs={{0,64},{64,0},{1,65},{65,1},{2,66},{66,2},{3,67},{67,3},{4,68},{68... | collective-permute-start | bytes 294920 | tf_op jit(solution)/shard_map/ppermute | solution.py:246
  7.4 0.0 copy-start.2
  7.4 9.8 %all-to-all-start = ((bf16[32,24,384]{2,1,0:T(8,128)(2,1)}), bf16[32,24,384]{2,1,0:T(8,128)(2,1)S(1)}, u32[]{:S(2)}, u32[]{:S(2)}) async-start(bf16[32,24,384]{2,1,0:T(8,128)(2,1)} %bitcast.8), calls=%async_computation | async-start | bytes 1179648 | tf_op jit(solution)/shard_map/all_to_all | solution.py:231
  17.3 0.0 collective-permute-done
  17.3 0.0 copy-done.2
  17.3 0.0 copy-start
  17.3 23.2 %all_gather.3.own = bf16[512,768]{1,0:T(8,128)(2,1)S(1)} all-gather(bf16[128,768]{1,0:T(8,128)(2,1)S(1)} %pad_maximum_fusion), channel_id=1, replica_groups=mesh['zq'=4,'zp'=2,'y'=4,'c'=2,'h'=2,'x'=4] {'zq'}, dimensions={0}, use_global_device_ids=true | all-gather | bytes 983040 | tf_op jit(solution)/shard_map/all_gather | solution.py:247
  40.5 0.0 copy-start.1
  40.5 5.0 %collective-permute-start.1 = (bf16[512,768]{1,0:T(8,128)(2,1)S(1)}, bf16[512,768]{1,0:T(8,128)(2,1)S(1)}, u32[]{:S(2)}, u32[]{:S(2)}) collective-permute-start(bf16[512,768]{1,0:T(8,128)(2,1)S(1)} %all_gather.3.own), channel_id=1, source_target_pairs={{0,8},{8,0},{1,9},{9,1},{2,10},{10,2},{3,11},{11,3},{4,12},{12,4},... | collective-permute-start | bytes 2359304 | tf_op jit(solution)/shard_map/ppermute | solution.py:248
  45.5 0.0 all-to-all-done
  45.5 0.0 copy-done
  45.5 0.0 copy-done.1
  45.5 2.2 %attend_own.1 = (f32[512,384]{1,0:T(8,128)S(1)}, f32[512,384]{1,0:T(8,128)S(1)}, f32[512,384]{1,0:T(8,128)S(1)}, f32[16,384]{1,0:T(8,128)S(1)}) custom-call(s32[2]{0:T(128)S(1)} %copy-done.1, bf16[8,4,24,384]{3,2,1,0:T(8,128)(2,1)S(1)} %bitcast.4, bf16[512,768]{1,0:T(8,128)(2,1)S(1)} %all_gather.3.own, f32[50,384]{1,0:T(8,128)S(1)} %copy-done), custom_call_target="tpu_custom_call" | custom-call | flops 402653184 | bytes 2097152 | tf_op jit(solution)/shard_map/attend_own/pallas_call | solution.py:251
  47.7 0.0 collective-permute-done.1.other
  47.7 1.8 %attend_other.1 = bf16[8,4,25,2,128]{4,3,2,1,0:T(2,128)(2,1)S(1)} custom-call(bf16[8,4,24,384]{3,2,1,0:T(8,128)(2,1)S(1)} %bitcast.5, bf16[512,768]{1,0:T(8,128)(2,1)S(1)} %collective-permute-done.1.other, f32[512,384]{1,0:T(8,128)S(1)} %get-tuple-element.10.acc_in, f32[512,384]{1,0:T(8,128)S(1)} %get-tuple-element.11.top_in, ...), custom_call_target="tpu_custom_call" | custom-call | flops 402653184 | bytes 2097152 | tf_op jit(solution)/shard_map/attend_other/pallas_call | solution.py:260
  49.5 24.5 %all_to_all.10 = bf16[32,25,2,128]{3,2,1,0:T(2,128)(2,1)S(1)} all-to-all(bf16[32,25,2,128]{3,2,1,0:T(2,128)(2,1)S(1)} %bitcast.7), channel_id=1, replica_groups=mesh['zq'=4,'zp'=2,'y'=4,'c'=2,'h'=2,'x'=4] {'h','x','y'}, dimensions={0} | all-to-all | bytes 819200 | tf_op jit(solution)/shard_map/all_to_all | solution.py:231
  74.1 1.3 %merge.1 = (bf16[8,3072]{1,0:T(8,128)(2,1)}, bf16[8,3072]{1,0:T(8,128)(2,1)}) custom-call(bf16[8,4,25,2,128]{4,3,2,1,0:T(2,128)(2,1)S(1)} %bitcast.6), custom_call_target="tpu_custom_call" | custom-call | tf_op jit(solution)/shard_map/merge/pallas_call | solution.py:270
  (1 shorter events, 0.0 us)
Async XLA Ops:
  2.6 14.7 %collective-permute-start = (bf16[64,768]{1,0:T(8,128)(2,1)}, bf16[64,768]{1,0:T(8,128)(2,1)S(1)}, u32[]{:S(2)}, u32[]{:S(2)}) collective-permute-start(bf16[64,768]{1,0:T(8,128)(2,1)} %get-tuple-element.9), channel_id=1, source_target_pairs={{0,64},{64,0},{1,65},{65,1},{2,66},{66,2},{3,67},{67,3},{4,68},{68... | collective-permute-start | bytes 294920 | tf_op jit(solution)/shard_map/ppermute | solution.py:246
  7.4 9.8 %copy-start.2 = (bf16[64,768]{1,0:T(8,128)(2,1)S(1)}, bf16[64,768]{1,0:T(8,128)(2,1)}, u32[]{:S(2)}) copy-start(bf16[64,768]{1,0:T(8,128)(2,1)} %get-tuple-element.9) | copy-start | bytes 294916
  7.4 38.0 %all-to-all-start = ((bf16[32,24,384]{2,1,0:T(8,128)(2,1)}), bf16[32,24,384]{2,1,0:T(8,128)(2,1)S(1)}, u32[]{:S(2)}, u32[]{:S(2)}) async-start(bf16[32,24,384]{2,1,0:T(8,128)(2,1)} %bitcast.8), calls=%async_computation | async-start | bytes 1179648 | tf_op jit(solution)/shard_map/all_to_all | solution.py:231
  17.3 28.2 %copy-start = (f32[50,384]{1,0:T(8,128)S(1)}, f32[50,384]{1,0:T(8,128)}, u32[]{:S(2)}) copy-start(f32[50,384]{1,0:T(8,128)} %gates.1) | copy-start | bytes 230404
  40.5 5.0 %copy-start.1 = (s32[2]{0:T(128)S(1)}, s32[2]{0:T(128)}, u32[]{:S(2)}) copy-start(s32[2]{0:T(128)} %step_ref.1) | copy-start | bytes 28
  40.5 7.2 %collective-permute-start.1 = (bf16[512,768]{1,0:T(8,128)(2,1)S(1)}, bf16[512,768]{1,0:T(8,128)(2,1)S(1)}, u32[]{:S(2)}, u32[]{:S(2)}) collective-permute-start(bf16[512,768]{1,0:T(8,128)(2,1)S(1)} %all_gather.3.own), channel_id=1, source_target_pairs={{0,8},{8,0},{1,9},{9,1},{2,10},{10,2},{3,11},{11,3},{4,12},{12,4},... | collective-permute-start | bytes 2359304 | tf_op jit(solution)/shard_map/ppermute | solution.py:248

commit v8 on v7

--- a/solution.py
+++ b/solution.py
@@ -173,9 +173,10 @@
         for y in range(NY):
             total = acc[patch_rows(y)] + keeps[y] * acc_in[patch_rows(y), cols]
             mixed = (total / totals[y]) * gate
-            out[:, y, head * TOK : (head + 1) * TOK, :, :] = (
-                mixed.astype(BF16).reshape(NHEAD, TOK, 2, HDIM)
-            )
+            mixed = mixed.astype(BF16)
+            for i in range(NHEAD):
+                start = 2 * SENT * (i * NY + y) + 2 * TOK * head
+                out[start : start + 2 * TOK, :] = mixed[2 * TOK * i : 2 * TOK * (i + 1)]
             size = tops[y] * SCALE2 + jnp.log(totals[y]) * (1.0 / LN2)
             for i, piece in enumerate(split3(size)):
                 stats[y] = jnp.where(slot == 3 * head + i, piece.astype(F32), stats[y])
@@ -184,7 +185,8 @@
             rows = stats[y][2 * TOK * i : 2 * TOK * i + TOK] + stats[y][2 * TOK * i + TOK : 2 * TOK * (i + 1)]
             rows = rows + pltpu.roll(rows, 4, 0)
             rows = rows + pltpu.roll(rows, 2, 0)
-            out[i, y, SENT - 1, :, :] = rows[0:2].astype(BF16)
+            start = 2 * SENT * (i * NY + y) + 2 * TOK * GROUP
+            out[start : start + 2, :] = rows[0:2].astype(BF16)
 
 
 def merge_kernel(recv, out_first, out_second):
@@ -193,7 +195,9 @@
     spread = jnp.where((at % (3 * GROUP)) // 3 == to // HDIM, 1.0, 0.0).astype(BF16)
     lane = lax.broadcasted_iota(jnp.int32, (ALL, HDIM), 1)
     pair = lax.broadcasted_iota(jnp.int32, (ALL, HDIM), 0) // 2 % TOK
-    stats = jnp.concatenate([recv[:, y, SENT - 1, :, :].reshape(2 * NHEAD, HDIM) for y in range(NY)], axis=0)
+    stats = jnp.concatenate(
+        [recv[pl.ds(2 * SENT * (i * NY + y + 1) - 2, 2), :] for y in range(NY) for i in range(NHEAD)], axis=0
+    )
     stats = jnp.dot(fold_matrix(ALL, 2 * PEERS, 1, 0), stats, preferred_element_type=F32)
     stats = jnp.where(lane // (3 * GROUP) == pair, stats, 0.0).astype(BF16)
     sizes = jnp.dot(stats, spread, preferred_element_type=F32)
@@ -205,7 +209,8 @@
         for y in range(NY):
             weight = jnp.exp2(size[y] - top)
             total = total + weight
-            part = recv[:, y, head * TOK : (head + 1) * TOK, :, :].reshape(ROWS, HDIM)
+            starts = [2 * SENT * (i * NY + y) + 2 * TOK * head for i in range(NHEAD)]
+            part = jnp.concatenate([recv[a : a + 2 * TOK, :] for a in starts], axis=0)
             acc = acc + weight * part.astype(F32)
         result = acc / total
         for g in range(NHEAD):
@@ -259,14 +264,14 @@
     )(step_index, recv, own, gate_table)
     partial = pl.pallas_call(
         attend_other_kernel,
-        out_shape=shape((NHEAD, NY, SENT, 2, HDIM), BF16),
+        out_shape=shape((2 * SENT * PEERS, HDIM), BF16),
         in_specs=vmem(6),
         out_specs=vmem(1)[0],
         compiler_params=PARAMS,
         cost_estimate=cost,
         name="attend_other",
     )(recv, other, *state)
-    back = exchange(partial)
+    back = exchange(partial.reshape((NHEAD, NY, SENT, 2, HDIM))).reshape(partial.shape)
     return pl.pallas_call(
         merge_kernel,
         out_shape=(shape((TOK, NHEAD * WIDTH), BF16),) * 2,

time: 75.8 us -> 75.5 us (level)
  no operation moved by 1% of the time
where the time goes in v8:
time: 75.5 us; the launch traced here: 75.1 us
  blocking collectives  47.7 us (63%)
  starting transfers between devices  19.6 us (26%)
  Pallas kernels  7.05 us (9%)
    all_to_all x1, blocking collectives, exchange(): lax.all_to_all(flat, PLANE, split_axis=0, concat_axis=0, tiled=True)  24.5 us
    all_gather x1, blocking collectives, body(): lax.all_gather(jnp.concatenate([kv, pair], axis=0), 'zq', axis=0, tiled=T...  23.2 us
    all_to_all x1, starting transfers between devices, exchange(): lax.all_to_all(flat, PLANE, split_axis=0, concat_axis=0, tiled=True)  9.81 us
    ppermute x1, starting transfers between devices, body(): other = lax.ppermute(own, 'c', [(0, 1), (1, 0)])  4.99 us
    ppermute x1, starting transfers between devices, body(): pair = lax.ppermute(kv, 'zp', [(0, 1), (1, 0)])  4.83 us
    pallas_call x1, Pallas kernels, body(): pl.pallas_call(attend_own_kernel, out_shape=state, in_specs=smem(1) + vme...  2.17 us
    pallas_call x1, Pallas kernels, body(): pl.pallas_call(pack_kernel, out_shape=(shape((NHEAD, NY, BLOCK, WIDTH), B...  1.96 us
    pallas_call x1, Pallas kernels, body(): pl.pallas_call(attend_other_kernel, out_shape=shape((2 * SENT * PEERS, HD...  1.72 us
  transfers between devices with their start and end apart: 3, of which 0 were waited for; matrix products, arithmetic and copies ran while one was open for 0% of the time, Pallas kernels for 3%

profile of v8, /device:TPU:1, one launch (start us, length us, event | category | flops | bytes accessed | tf_op | source)
XLA Modules:
  0.0 75.1 jit_solution(14431638061800179988)
XLA Ops:
  0.6 2.0 %pack.1 = (bf16[8,4,24,384]{3,2,1,0:T(8,128)(2,1)}, bf16[64,768]{1,0:T(8,128)(2,1)}) custom-call(bf16[8,3072]{1,0:T(8,128)(2,1)} %q1.1, bf16[8,3072]{1,0:T(8,128)(2,1)} %k1.1, bf16[8,3072]{1,0:T(8,128)(2,1)} %v1.1, bf16[8,3072]{1,0:T(8,128)(2,1)} %q2.1, bf16[8,3072]{1,0:T(8,128)(2,1)} %k2.1, bf16[8,3072]{1,0:T(8,128)(2,1)} %v2.1, bf16[64,384]{1,0:T(8,128)(2,1)} %ks.1, ...), custom_call_target="tpu_custom_call" | custom-call | tf_op jit(solution)/shard_map/pack/pallas_call | solution.py:241
  2.6 4.8 %collective-permute-start = (bf16[64,768]{1,0:T(8,128)(2,1)}, bf16[64,768]{1,0:T(8,128)(2,1)S(1)}, u32[]{:S(2)}, u32[]{:S(2)}) collective-permute-start(bf16[64,768]{1,0:T(8,128)(2,1)} %get-tuple-element.9), channel_id=1, source_target_pairs={{0,64},{64,0},{1,65},{65,1},{2,66},{66,2},{3,67},{67,3},{4,68},{68... | collective-permute-start | bytes 294920 | tf_op jit(solution)/shard_map/ppermute | solution.py:251
  7.4 0.0 copy-start.2
  7.4 9.8 %all-to-all-start = ((bf16[32,24,384]{2,1,0:T(8,128)(2,1)}), bf16[32,24,384]{2,1,0:T(8,128)(2,1)S(1)}, u32[]{:S(2)}, u32[]{:S(2)}) async-start(bf16[32,24,384]{2,1,0:T(8,128)(2,1)} %bitcast.8), calls=%async_computation | async-start | bytes 1179648 | tf_op jit(solution)/shard_map/all_to_all | solution.py:236
  17.3 0.0 collective-permute-done
  17.3 0.0 copy-done.2
  17.3 0.0 copy-start
  17.3 23.2 %all_gather.3.own = bf16[512,768]{1,0:T(8,128)(2,1)S(1)} all-gather(bf16[128,768]{1,0:T(8,128)(2,1)S(1)} %pad_maximum_fusion), channel_id=1, replica_groups=mesh['zq'=4,'zp'=2,'y'=4,'c'=2,'h'=2,'x'=4] {'zq'}, dimensions={0}, use_global_device_ids=true | all-gather | bytes 983040 | tf_op jit(solution)/shard_map/all_gather | solution.py:252
  40.5 0.0 copy-start.1
  40.5 5.0 %collective-permute-start.1 = (bf16[512,768]{1,0:T(8,128)(2,1)S(1)}, bf16[512,768]{1,0:T(8,128)(2,1)S(1)}, u32[]{:S(2)}, u32[]{:S(2)}) collective-permute-start(bf16[512,768]{1,0:T(8,128)(2,1)S(1)} %all_gather.3.own), channel_id=1, source_target_pairs={{0,8},{8,0},{1,9},{9,1},{2,10},{10,2},{3,11},{11,3},{4,12},{12,4},... | collective-permute-start | bytes 2359304 | tf_op jit(solution)/shard_map/ppermute | solution.py:253
  45.5 0.0 all-to-all-done
  45.5 0.0 copy-done
  45.5 0.0 copy-done.1
  45.5 2.2 %attend_own.1 = (f32[512,384]{1,0:T(8,128)S(1)}, f32[512,384]{1,0:T(8,128)S(1)}, f32[512,384]{1,0:T(8,128)S(1)}, f32[16,384]{1,0:T(8,128)S(1)}) custom-call(s32[2]{0:T(128)S(1)} %copy-done.1, bf16[8,4,24,384]{3,2,1,0:T(8,128)(2,1)S(1)} %bitcast.4, bf16[512,768]{1,0:T(8,128)(2,1)S(1)} %all_gather.3.own, f32[50,384]{1,0:T(8,128)S(1)} %copy-done), custom_call_target="tpu_custom_call" | custom-call | flops 402653184 | bytes 2097152 | tf_op jit(solution)/shard_map/attend_own/pallas_call | solution.py:256
  47.7 0.0 collective-permute-done.1.other
  47.7 1.7 %attend_other.1 = bf16[1600,128]{1,0:T(8,128)(2,1)S(1)} custom-call(bf16[8,4,24,384]{3,2,1,0:T(8,128)(2,1)S(1)} %bitcast.5, bf16[512,768]{1,0:T(8,128)(2,1)S(1)} %collective-permute-done.1.other, f32[512,384]{1,0:T(8,128)S(1)} %get-tuple-element.10.acc_in, f32[512,384]{1,0:T(8,128)S(1)} %get-tuple-element.11.top_in, ...), custom_call_target="tpu_custom_call" | custom-call | flops 402653184 | bytes 2097152 | tf_op jit(solution)/shard_map/attend_other/pallas_call | solution.py:265
  49.4 24.5 %all_to_all.10 = bf16[32,25,2,128]{3,2,1,0:T(2,128)(2,1)S(1)} all-to-all(bf16[32,25,2,128]{3,2,1,0:T(2,128)(2,1)S(1)} %bitcast.7), channel_id=1, replica_groups=mesh['zq'=4,'zp'=2,'y'=4,'c'=2,'h'=2,'x'=4] {'h','x','y'}, dimensions={0} | all-to-all | bytes 819200 | tf_op jit(solution)/shard_map/all_to_all | solution.py:236
  73.9 1.2 %merge.1 = (bf16[8,3072]{1,0:T(8,128)(2,1)}, bf16[8,3072]{1,0:T(8,128)(2,1)}) custom-call(bf16[1600,128]{1,0:T(8,128)(2,1)S(1)} %bitcast.6), custom_call_target="tpu_custom_call" | custom-call | tf_op jit(solution)/shard_map/merge/pallas_call | solution.py:275
  (1 shorter events, 0.0 us)
Async XLA Ops:
  2.6 14.7 %collective-permute-start = (bf16[64,768]{1,0:T(8,128)(2,1)}, bf16[64,768]{1,0:T(8,128)(2,1)S(1)}, u32[]{:S(2)}, u32[]{:S(2)}) collective-permute-start(bf16[64,768]{1,0:T(8,128)(2,1)} %get-tuple-element.9), channel_id=1, source_target_pairs={{0,64},{64,0},{1,65},{65,1},{2,66},{66,2},{3,67},{67,3},{4,68},{68... | collective-permute-start | bytes 294920 | tf_op jit(solution)/shard_map/ppermute | solution.py:251
  7.4 9.8 %copy-start.2 = (bf16[64,768]{1,0:T(8,128)(2,1)S(1)}, bf16[64,768]{1,0:T(8,128)(2,1)}, u32[]{:S(2)}) copy-start(bf16[64,768]{1,0:T(8,128)(2,1)} %get-tuple-element.9) | copy-start | bytes 294916
  7.4 38.0 %all-to-all-start = ((bf16[32,24,384]{2,1,0:T(8,128)(2,1)}), bf16[32,24,384]{2,1,0:T(8,128)(2,1)S(1)}, u32[]{:S(2)}, u32[]{:S(2)}) async-start(bf16[32,24,384]{2,1,0:T(8,128)(2,1)} %bitcast.8), calls=%async_computation | async-start | bytes 1179648 | tf_op jit(solution)/shard_map/all_to_all | solution.py:236
  17.3 28.2 %copy-start = (f32[50,384]{1,0:T(8,128)S(1)}, f32[50,384]{1,0:T(8,128)}, u32[]{:S(2)}) copy-start(f32[50,384]{1,0:T(8,128)} %gates.1) | copy-start | bytes 230404
  40.5 5.0 %copy-start.1 = (s32[2]{0:T(128)S(1)}, s32[2]{0:T(128)}, u32[]{:S(2)}) copy-start(s32[2]{0:T(128)} %step_ref.1) | copy-start | bytes 28
  40.5 7.2 %collective-permute-start.1 = (bf16[512,768]{1,0:T(8,128)(2,1)S(1)}, bf16[512,768]{1,0:T(8,128)(2,1)S(1)}, u32[]{:S(2)}, u32[]{:S(2)}) collective-permute-start(bf16[512,768]{1,0:T(8,128)(2,1)S(1)} %all_gather.3.own), channel_id=1, source_target_pairs={{0,8},{8,0},{1,9},{9,1},{2,10},{10,2},{3,11},{11,3},{4,12},{12,4},... | collective-permute-start | bytes 2359304 | tf_op jit(solution)/shard_map/ppermute | solution.py:253

commit v9 on v7

--- a/solution.py
+++ b/solution.py
@@ -108,13 +108,14 @@
 
     def scores(head):
         q = queries_of(recv, head)
+        main = nt_dot(q, own[:, head_cols(head)])
         extra = []
         for y in range(NY):
             fresh = recv[:, y, 2 * TOK : BLOCK, head_cols(head)].astype(F32)
             fresh = fresh.reshape(FRESH_ROWS, HDIM).astype(BF16)
             fresh_v = jnp.dot(shift, fresh, preferred_element_type=F32).astype(BF16)
             extra.append((nt_dot(q[patch_rows(y)], fresh) + fresh_bias, fresh_v))
-        return nt_dot(q, own[:, head_cols(head)]), extra
+        return main, extra
 
     ready = scores(0)
     for head in range(GROUP):

time: 75.8 us -> 75.9 us (level)
  no operation moved by 1% of the time
where the time goes in v9:
time: 75.9 us; the launch traced here: 75.5 us
  blocking collectives  47.7 us (63%)
  starting transfers between devices  19.6 us (26%)
  Pallas kernels  7.41 us (10%)
    all_to_all x1, blocking collectives, exchange(): lax.all_to_all(flat, PLANE, split_axis=0, concat_axis=0, tiled=True)  24.6 us
    all_gather x1, blocking collectives, body(): lax.all_gather(jnp.concatenate([kv, pair], axis=0), 'zq', axis=0, tiled=T...  23.2 us
    all_to_all x1, starting transfers between devices, exchange(): lax.all_to_all(flat, PLANE, split_axis=0, concat_axis=0, tiled=True)  9.81 us
    ppermute x1, starting transfers between devices, body(): other = lax.ppermute(own, 'c', [(0, 1), (1, 0)])  4.99 us
    ppermute x1, starting transfers between devices, body(): pair = lax.ppermute(kv, 'zp', [(0, 1), (1, 0)])  4.83 us
    pallas_call x1, Pallas kernels, body(): pl.pallas_call(attend_own_kernel, out_shape=state, in_specs=smem(1) + vme...  2.28 us
    pallas_call x1, Pallas kernels, body(): pl.pallas_call(pack_kernel, out_shape=(shape((NHEAD, NY, BLOCK, WIDTH), B...  1.96 us
    pallas_call x1, Pallas kernels, body(): pl.pallas_call(attend_other_kernel, out_shape=shape((NHEAD, NY, SENT, 2,...  1.86 us
  transfers between devices with their start and end apart: 3, of which 0 were waited for; matrix products, arithmetic and copies ran while one was open for 0% of the time, Pallas kernels for 3%

profile of v9, /device:TPU:1, one launch (start us, length us, event | category | flops | bytes accessed | tf_op | source)
XLA Modules:
  0.0 75.5 jit_solution(4598008154283148556)
XLA Ops:
  0.6 2.0 %pack.1 = (bf16[8,4,24,384]{3,2,1,0:T(8,128)(2,1)}, bf16[64,768]{1,0:T(8,128)(2,1)}) custom-call(bf16[8,3072]{1,0:T(8,128)(2,1)} %q1.1, bf16[8,3072]{1,0:T(8,128)(2,1)} %k1.1, bf16[8,3072]{1,0:T(8,128)(2,1)} %v1.1, bf16[8,3072]{1,0:T(8,128)(2,1)} %q2.1, bf16[8,3072]{1,0:T(8,128)(2,1)} %k2.1, bf16[8,3072]{1,0:T(8,128)(2,1)} %v2.1, bf16[64,384]{1,0:T(8,128)(2,1)} %ks.1, ...), custom_call_target="tpu_custom_call" | custom-call | tf_op jit(solution)/shard_map/pack/pallas_call | solution.py:237
  2.6 4.8 %collective-permute-start = (bf16[64,768]{1,0:T(8,128)(2,1)}, bf16[64,768]{1,0:T(8,128)(2,1)S(1)}, u32[]{:S(2)}, u32[]{:S(2)}) collective-permute-start(bf16[64,768]{1,0:T(8,128)(2,1)} %get-tuple-element.9), channel_id=1, source_target_pairs={{0,64},{64,0},{1,65},{65,1},{2,66},{66,2},{3,67},{67,3},{4,68},{68... | collective-permute-start | bytes 294920 | tf_op jit(solution)/shard_map/ppermute | solution.py:247
  7.4 0.0 copy-start.2
  7.4 9.8 %all-to-all-start = ((bf16[32,24,384]{2,1,0:T(8,128)(2,1)}), bf16[32,24,384]{2,1,0:T(8,128)(2,1)S(1)}, u32[]{:S(2)}, u32[]{:S(2)}) async-start(bf16[32,24,384]{2,1,0:T(8,128)(2,1)} %bitcast.8), calls=%async_computation | async-start | bytes 1179648 | tf_op jit(solution)/shard_map/all_to_all | solution.py:232
  17.3 0.0 collective-permute-done
  17.3 0.0 copy-done.2
  17.3 0.0 copy-start
  17.3 23.2 %all_gather.3.own = bf16[512,768]{1,0:T(8,128)(2,1)S(1)} all-gather(bf16[128,768]{1,0:T(8,128)(2,1)S(1)} %pad_maximum_fusion), channel_id=1, replica_groups=mesh['zq'=4,'zp'=2,'y'=4,'c'=2,'h'=2,'x'=4] {'zq'}, dimensions={0}, use_global_device_ids=true | all-gather | bytes 983040 | tf_op jit(solution)/shard_map/all_gather | solution.py:248
  40.5 0.0 copy-start.1
  40.5 5.0 %collective-permute-start.1 = (bf16[512,768]{1,0:T(8,128)(2,1)S(1)}, bf16[512,768]{1,0:T(8,128)(2,1)S(1)}, u32[]{:S(2)}, u32[]{:S(2)}) collective-permute-start(bf16[512,768]{1,0:T(8,128)(2,1)S(1)} %all_gather.3.own), channel_id=1, source_target_pairs={{0,8},{8,0},{1,9},{9,1},{2,10},{10,2},{3,11},{11,3},{4,12},{12,4},... | collective-permute-start | bytes 2359304 | tf_op jit(solution)/shard_map/ppermute | solution.py:249
  45.5 0.0 all-to-all-done
  45.5 0.0 copy-done
  45.5 0.0 copy-done.1
  45.5 2.3 %attend_own.1 = (f32[512,384]{1,0:T(8,128)S(1)}, f32[512,384]{1,0:T(8,128)S(1)}, f32[512,384]{1,0:T(8,128)S(1)}, f32[16,384]{1,0:T(8,128)S(1)}) custom-call(s32[2]{0:T(128)S(1)} %copy-done.1, bf16[8,4,24,384]{3,2,1,0:T(8,128)(2,1)S(1)} %bitcast.4, bf16[512,768]{1,0:T(8,128)(2,1)S(1)} %all_gather.3.own, f32[50,384]{1,0:T(8,128)S(1)} %copy-done), custom_call_target="tpu_custom_call" | custom-call | flops 402653184 | bytes 2097152 | tf_op jit(solution)/shard_map/attend_own/pallas_call | solution.py:252
  47.8 0.0 collective-permute-done.1.other
  47.8 1.9 %attend_other.1 = bf16[8,4,25,2,128]{4,3,2,1,0:T(2,128)(2,1)S(1)} custom-call(bf16[8,4,24,384]{3,2,1,0:T(8,128)(2,1)S(1)} %bitcast.5, bf16[512,768]{1,0:T(8,128)(2,1)S(1)} %collective-permute-done.1.other, f32[512,384]{1,0:T(8,128)S(1)} %get-tuple-element.10.acc_in, f32[512,384]{1,0:T(8,128)S(1)} %get-tuple-element.11.top_in, ...), custom_call_target="tpu_custom_call" | custom-call | flops 402653184 | bytes 2097152 | tf_op jit(solution)/shard_map/attend_other/pallas_call | solution.py:261
  49.7 24.6 %all_to_all.10 = bf16[32,25,2,128]{3,2,1,0:T(2,128)(2,1)S(1)} all-to-all(bf16[32,25,2,128]{3,2,1,0:T(2,128)(2,1)S(1)} %bitcast.7), channel_id=1, replica_groups=mesh['zq'=4,'zp'=2,'y'=4,'c'=2,'h'=2,'x'=4] {'h','x','y'}, dimensions={0} | all-to-all | bytes 819200 | tf_op jit(solution)/shard_map/all_to_all | solution.py:232
  74.2 1.3 %merge.1 = (bf16[8,3072]{1,0:T(8,128)(2,1)}, bf16[8,3072]{1,0:T(8,128)(2,1)}) custom-call(bf16[8,4,25,2,128]{4,3,2,1,0:T(2,128)(2,1)S(1)} %bitcast.6), custom_call_target="tpu_custom_call" | custom-call | tf_op jit(solution)/shard_map/merge/pallas_call | solution.py:271
  (1 shorter events, 0.0 us)
Async XLA Ops:
  2.6 14.7 %collective-permute-start = (bf16[64,768]{1,0:T(8,128)(2,1)}, bf16[64,768]{1,0:T(8,128)(2,1)S(1)}, u32[]{:S(2)}, u32[]{:S(2)}) collective-permute-start(bf16[64,768]{1,0:T(8,128)(2,1)} %get-tuple-element.9), channel_id=1, source_target_pairs={{0,64},{64,0},{1,65},{65,1},{2,66},{66,2},{3,67},{67,3},{4,68},{68... | collective-permute-start | bytes 294920 | tf_op jit(solution)/shard_map/ppermute | solution.py:247
  7.4 9.8 %copy-start.2 = (bf16[64,768]{1,0:T(8,128)(2,1)S(1)}, bf16[64,768]{1,0:T(8,128)(2,1)}, u32[]{:S(2)}) copy-start(bf16[64,768]{1,0:T(8,128)(2,1)} %get-tuple-element.9) | copy-start | bytes 294916
  7.4 38.0 %all-to-all-start = ((bf16[32,24,384]{2,1,0:T(8,128)(2,1)}), bf16[32,24,384]{2,1,0:T(8,128)(2,1)S(1)}, u32[]{:S(2)}, u32[]{:S(2)}) async-start(bf16[32,24,384]{2,1,0:T(8,128)(2,1)} %bitcast.8), calls=%async_computation | async-start | bytes 1179648 | tf_op jit(solution)/shard_map/all_to_all | solution.py:232
  17.3 28.2 %copy-start = (f32[50,384]{1,0:T(8,128)S(1)}, f32[50,384]{1,0:T(8,128)}, u32[]{:S(2)}) copy-start(f32[50,384]{1,0:T(8,128)} %gates.1) | copy-start | bytes 230404
  40.5 5.0 %copy-start.1 = (s32[2]{0:T(128)S(1)}, s32[2]{0:T(128)}, u32[]{:S(2)}) copy-start(s32[2]{0:T(128)} %step_ref.1) | copy-start | bytes 28
  40.5 7.3 %collective-permute-start.1 = (bf16[512,768]{1,0:T(8,128)(2,1)S(1)}, bf16[512,768]{1,0:T(8,128)(2,1)S(1)}, u32[]{:S(2)}, u32[]{:S(2)}) collective-permute-start(bf16[512,768]{1,0:T(8,128)(2,1)S(1)} %all_gather.3.own), channel_id=1, source_target_pairs={{0,8},{8,0},{1,9},{9,1},{2,10},{10,2},{3,11},{11,3},{4,12},{12,4},... | collective-permute-start | bytes 2359304 | tf_op jit(solution)/shard_map/ppermute | solution.py:249
